TPU v7x, 128 devices: a whole 4x4x4 slice. The times are simulated.
128 devices in a mesh: rows: 16 (over z, x), table: 8 (over y, core).
Axes of the slice: x: 4, y: 4, z: 4, core: 2. Of those that a mesh axis runs over, the one named last changes fastest.
Arguments:
- item_table: bfloat16 [2097152, 128], P(('rows', 'table')), may hold values from -40 to 40, as said below
- user_rows: float32 [8192, 128], P(('rows', 'table')), may hold values from -3 to 3
- link_rows: int32 [8192, 128], P(('rows', 'table')), may hold values from 0 to 16383
- link_slots: int32 [8192, 128], P(('rows', 'table')), may hold values from 0 to 8191, as said below
- link_weights: int32 [8192, 128], P(('rows', 'table')), may hold values from 1 to 63
- link_counts: int32 [8192], P(('rows', 'table')), may hold values from 1 to 128
Outputs:
- solved_rows: float32 [8192, 128], P(('rows', 'table'))
Inputs may be any that keep to these rules, and one draw needn't show every extreme that they name: `item_table`: rows differ in scale; values lie within the stated bounds. `link_slots`: on each device (flat index over rows then table, users in blocks of 64), its 8192 entries hold every number of 0 to 8191 exactly once; entry s names slot s % 64 toward the device of flat index s // 64, which holds the linked item, so every device names exactly 64 slots of every owner, live or not.
All inputs are finite; a program needn't handle non-finite values.
Results may differ from a plain program's by a relative error of at most 0.0019.
Values may be sent and summed in bfloat16 or wider, within the bound.
No kernel may reach another device: no remote copies, remote signals or barrier semaphores. Data moves between devices by JAX's collectives and lax.ppermute only.
A program may use at most 64 MiB of HBM per device.

v0:
```python
import math

import jax
import jax.numpy as jnp
from jax import lax
from jax.sharding import PartitionSpec as P

CG_STEPS = 3


def refine(apply_system, target, initial):
    estimate = initial
    residual = target - apply_system(estimate)
    direction = residual
    norm_now = jnp.sum(residual * residual, axis=1, keepdims=True)
    for iteration in range(CG_STEPS):
        image = apply_system(direction)
        curvature = jnp.sum(direction * image, axis=1, keepdims=True)
        step_len = norm_now / (curvature + 1e-06)
        estimate = estimate + step_len * direction
        residual = residual - step_len * image
        norm_next = jnp.sum(residual * residual, axis=1, keepdims=True)
        direction = residual + norm_next / (norm_now + 1e-06) * direction
        norm_now = norm_next
    return estimate


def place_requests(slots_flat, rows_flat, block_rows):
    total = slots_flat.shape[0]
    row_pair = jnp.stack([rows_flat // 128, rows_flat % 128], axis=1).astype(jnp.bfloat16)

    def place_one_block(start):
        wanted = start + jnp.arange(block_rows, dtype=jnp.int32)
        selector = (wanted[:, None] == slots_flat[None, :]).astype(jnp.bfloat16)
        picked = jnp.dot(selector, row_pair, preferred_element_type=jnp.float32).astype(jnp.int32)
        return picked[:, 0] * 128 + picked[:, 1]

    starts = jnp.arange(total // block_rows, dtype=jnp.int32) * block_rows
    return lax.map(place_one_block, starts).reshape(total)


def order_rows(slots_flat, arrived, block_rows):
    total = slots_flat.shape[0]
    positions = jnp.arange(total, dtype=jnp.int32)

    def order_one_block(slot_block):
        selector = (slot_block[:, None] == positions[None, :]).astype(jnp.bfloat16)
        return jnp.dot(selector, arrived, preferred_element_type=jnp.float32).astype(jnp.bfloat16)

    return lax.map(order_one_block, slots_flat.reshape(total // block_rows, block_rows)).reshape(
        total, arrived.shape[1]
    )


def per_device(item_table, user_rows, link_rows, link_slots, link_weights, link_counts):
    user_count, features = user_rows.shape
    slot_count = link_rows.shape[1]
    row_groups = lax.axis_size("rows")
    table_groups = lax.axis_size("table")
    devices = row_groups * table_groups
    capacity = user_count * slot_count // devices
    total_items = item_table.shape[0] * devices
    link_total = user_count * slot_count
    block_rows = math.gcd(link_total, 512)
    partial_value = jnp.dot(item_table.T, item_table, preferred_element_type=jnp.float32)
    gramian = lax.psum(partial_value, ("rows", "table"))
    shared = gramian * (slot_count / total_items) + 0.5 * slot_count * jnp.eye(
        features, dtype=jnp.float32
    )
    slots_flat = link_slots.reshape(link_total)
    requests = place_requests(slots_flat, link_rows.reshape(link_total), block_rows)
    outgoing = requests.reshape(devices, capacity)
    arrived = lax.all_to_all(
        item_table[
            lax.all_to_all(outgoing, ("rows", "table"), split_axis=0, concat_axis=0, tiled=True)
        ],
        ("rows", "table"),
        split_axis=0,
        concat_axis=0,
        tiled=True,
    )
    arrived = arrived.reshape(link_total, features)
    fetched = order_rows(slots_flat, arrived, block_rows)
    block_size = math.gcd(user_count, 64)
    block_count = user_count // block_size

    def solve_block(pieces):
        rows_block, weight_block, count_block, start_block = pieces
        live_mask = jnp.arange(slot_count, dtype=jnp.int32)[None, :] < count_block[:, None]
        confidence = jnp.where(live_mask, 1.0 + weight_block.astype(jnp.float32) / 8.0, 0.0)
        scaled = (confidence[:, :, None] * rows_block.astype(jnp.float32)).astype(jnp.bfloat16)
        target = jnp.sum(scaled.astype(jnp.float32), axis=1)
        weighted = jnp.einsum(
            "ulk,ulm->ukm", scaled, rows_block, preferred_element_type=jnp.float32
        )
        system = shared[None, :, :] + weighted

        def apply_system(vector):
            return jnp.einsum("ukm,um->uk", system, vector, precision=lax.Precision.HIGHEST)

        return refine(apply_system, target, start_block)

    solved = lax.map(
        solve_block,
        (
            fetched.reshape(block_count, block_size, slot_count, features),
            link_weights.reshape(block_count, block_size, slot_count),
            link_counts.reshape(block_count, block_size),
            user_rows.reshape(block_count, block_size, features),
        ),
    )
    return solved.reshape(user_count, features)


def solution(mesh):
    placed = (
        P(("rows", "table"), None),
        P(("rows", "table"), None),
        P(("rows", "table"), None),
        P(("rows", "table"), None),
        P(("rows", "table"), None),
        P(("rows", "table")),
    )
    return jax.shard_map(
        per_device,
        mesh=mesh,
        in_specs=placed,
        out_specs=P(("rows", "table"), None),
        check_vma=False,
    )
```

profile of v0, /device:TPU:1, one launch (start us, length us, event | category | flops | bytes accessed | tf_op | source)
XLA Modules:
  0.0 391.0 jit_solution(13837542746840187659)
XLA Ops:
  7.6 77.5 %while.25 = (s32[]{:T(128)}, s32[16,512]{1,0:T(8,128)S(1)}, s32[16]{0:T(128)S(1)}, s32[64,128]{1,0:T(8,128)}, bf16[8192,2]{0,1:T(2,128)(2,1)S(1)}, /*index=5*/s32[]{:T(128)}, s32[]{:T(128)}) while((s32[]{:T(128)}, s32[16,512]{1,0:T(8,128)S(1)}, s32[16]{0:T(128)S(1)}, s32[64,128]{1,0:T(8,128)}, bf16[8192,2]{0,1:T(2,128)(2,1)S(1)}, ...), condition=%wide.region_1.2_spmd, body=%wide.region_0.0_spmd.sunk | while | flops 20974080 | bytes 84065 | solution.py:39
  85.2 20.9 %all_to_all.17 = s32[128,1,64]{2,1,0:T(1,128)S(1)} all-to-all(s32[128,1,64]{2,1,0:T(1,128)S(1)} %bitcast.71), channel_id=1, replica_groups=mesh['rows'=16,'table'=8] {'rows','table'}, dimensions={0} | all-to-all | bytes 65536 | tf_op jit(solution)/shard_map/all_to_all | solution.py:75
  106.2 30.7 %gather_fusion = bf16[8192,128]{1,0:T(8,128)(2,1)} fusion(bf16[16384,128]{1,0:T(8,128)(2,1)} %param.10, s32[8192]{0:T(1024)S(1)} %broadcast_clamp_fusion), kind=kCustom, calls=%fused_computation | custom fusion | bytes 4227072 | tf_op jit(solution)/shard_map/gather | solution.py:74
  137.0 4.4 %all-to-all-start.1 = ((bf16[128,64,128]{2,1,0:T(8,128)(2,1)}), bf16[128,64,128]{2,1,0:T(8,128)(2,1)S(1)}, u32[]{:S(2)}, u32[]{:S(2)}) async-start(bf16[128,64,128]{2,1,0:T(8,128)(2,1)} %bitcast.6), calls=%async_computation.1 | async-start | bytes 4194304 | tf_op jit(solution)/shard_map/all_to_all | solution.py:73
  141.4 5.4 %fusion.30 = f32[128,128]{1,0:T(8,128)} fusion(bf16[16384,128]{1,0:T(8,128)(2,1)} %param.10), kind=kOutput, calls=%fused_computation.64 | convolution fusion | flops 536870912 | bytes 4259840 | tf_op jit(solution)/shard_map/dot_general | solution.py:65
  147.0 144.7 %all-reduce.2.cloned.1.call-done = f32[128,128]{1,0:T(8,128)} async-done(((f32[128,128]{1,0:T(8,128)}), f32[128,128]{1,0:T(8,128)}) %all-reduce.2.cloned.1.call-update) | async-done | bytes 65552 | tf_op jit(solution)/shard_map/psum | solution.py:66
  292.5 56.4 %while.26 = (s32[]{:T(128)}, bf16[16,512,128]{2,1,0:T(8,128)(2,1)}, s32[16,512]{1,0:T(8,128)S(1)}, bf16[8192,128]{1,0:T(8,128)(2,1)S(1)}, s32[]{:T(128)}) while((s32[]{:T(128)}, bf16[16,512,128]{2,1,0:T(8,128)(2,1)}, s32[16,512]{1,0:T(8,128)S(1)}, bf16[8192,128]{1,0:T(8,128)(2,1)S(1)}, s32[]{:T(128)}) %tuple.47), condition=%wide.region_3.4_spmd.clone, body=%wide.region_2.3_spmd.clone.sunk | while | flops 1078001664 | bytes 2234945 | solution.py:50
  292.5 3.5 fusion.51
  296.0 3.5 fusion.51
  299.6 3.5 fusion.51
  303.1 3.5 fusion.51
  310.1 3.5 fusion.51
  313.7 3.5 fusion.51
  317.2 3.5 fusion.51
  320.7 3.5 fusion.51
  324.2 3.5 fusion.51
  327.8 3.5 fusion.51
  331.3 3.5 fusion.51
  338.3 3.5 fusion.51
  345.4 3.5 fusion.51
  355.8 6.6 %fusion.21 = f32[64,1,128]{2,1,0:T(1,128)S(1)} fusion(f32[64,128,1]{1,2,0:T(1,128)S(1)} %bitcast.73, f32[64,128,128]{2,1,0:T(8,128)S(1)} %fusion.27, f32[128,128]{1,0:T(8,128)S(1)} %select_add_fusion), kind=kOutput, calls=%fused_computation.26 | convolution fusion | flops 13631488 | bytes 4325376 | tf_op jit(solution)/shard_map/while/body/eval_jaxpr/ukm,um->uk/dot_general | solution.py:99
  362.4 6.6 %fusion.19 = f32[64,1,128]{2,1,0:T(1,128)S(1)} fusion(f32[64,128,1]{1,2,0:T(1,128)S(1)} %bitcast.63, f32[64,128,128]{2,1,0:T(8,128)S(1)} %fusion.27, f32[128,128]{1,0:T(8,128)S(1)} %select_add_fusion), kind=kOutput, calls=%fused_computation.24 | convolution fusion | flops 13631488 | bytes 4325376 | tf_op jit(solution)/shard_map/while/body/eval_jaxpr/ukm,um->uk/dot_general | solution.py:99
  369.4 6.8 %fusion.17 = f32[64,1,128]{2,1,0:T(1,128)S(1)} fusion(f32[64,128,1]{1,2,0:T(1,128)S(1)} %bitcast.64, f32[64,128,128]{2,1,0:T(8,128)S(1)} %fusion.27, f32[128,128]{1,0:T(8,128)S(1)} %select_add_fusion), kind=kOutput, calls=%fused_computation.22 | convolution fusion | flops 13631488 | bytes 4325376 | tf_op jit(solution)/shard_map/while/body/eval_jaxpr/ukm,um->uk/dot_general | solution.py:99
  376.7 6.6 %fusion.15 = f32[64,1,128]{2,1,0:T(1,128)S(1)} fusion(f32[64,128,1]{1,2,0:T(1,128)S(1)} %bitcast.65, f32[64,128,128]{2,1,0:T(8,128)S(1)} %fusion.27, f32[128,128]{1,0:T(8,128)S(1)} %select_add_fusion), kind=kOutput, calls=%fused_computation.20 | convolution fusion | flops 13631488 | bytes 4325376 | tf_op jit(solution)/shard_map/while/body/eval_jaxpr/ukm,um->uk/dot_general | solution.py:99
  (140 shorter events, 98.3 us)
Async XLA Ops:
  137.0 155.5 %all-to-all-start.1 = ((bf16[128,64,128]{2,1,0:T(8,128)(2,1)}), bf16[128,64,128]{2,1,0:T(8,128)(2,1)S(1)}, u32[]{:S(2)}, u32[]{:S(2)}) async-start(bf16[128,64,128]{2,1,0:T(8,128)(2,1)} %bitcast.6), calls=%async_computation.1 | async-start | bytes 4194304 | tf_op jit(solution)/shard_map/all_to_all | solution.py:73
  141.4 5.5 %copy-start.1 = (s32[64,128]{1,0:T(8,128)S(1)}, s32[64,128]{1,0:T(8,128)}, u32[]{:S(2)}) copy-start(s32[64,128]{1,0:T(8,128)} %param.14) | copy-start | bytes 98308
  141.4 5.5 %copy-start.3 = (s32[64]{0:T(128)S(1)}, s32[64]{0:T(128)}, u32[]{:S(2)}) copy-start(s32[64]{0:T(128)} %param.15) | copy-start | bytes 772
  141.4 5.6 %copy-start.2 = (s32[64,128]{1,0:T(8,128)S(1)}, s32[64,128]{1,0:T(8,128)}, u32[]{:S(2)}) copy-start(s32[64,128]{1,0:T(8,128)} %get-tuple-element.213) | copy-start | bytes 98308
  141.4 150.2 %all-reduce.2.cloned.1.call-start = ((), (), s32[]{:S(2)}) async-start(), calls=%async_computation.2 | async-start | bytes 131072 | tf_op jit(solution)/shard_map/psum | solution.py:66
  352.3 3.5 copy-start
Sparse Core Ops, SparseCore 0:
  147.0 144.6 all-reduce.1
where the time goes:
time: 393 us; the launch traced here: 391 us
  matrix products  145 us (37%)
  waiting for transfers between devices  145 us (37%)
  local copies, waits for them, and re-layouts  46.1 us (12%)
  blocking collectives  20.9 us (5%)
  other arithmetic  16 us (4%)
  between operations  13.6 us (3%)
  starting transfers between devices  4.43 us (1%)
    psum x1, waiting for transfers between devices, per_device(): gramian = lax.psum(partial_value, ('rows', 'table'))  145 us
    dot_general x16, matrix products, order_one_block(): jnp.dot(selector, arrived, preferred_element_type=jnp.float32)  56.3 us
    dot_general x16, matrix products, place_one_block(): jnp.dot(selector, row_pair, preferred_element_type=jnp.float32)  54 us
    gather x1, local copies, waits for them, and re-layouts, per_device(): item_table[lax.all_to_all(outgoing, ('rows', 'table'), split_axis=0, conc...  30.7 us
    dot_general x4, matrix products, apply_system(): jnp.einsum('ukm,um->uk', system, vector, precision=lax.Precision.HIGHEST)  26.6 us
    all_to_all x1, blocking collectives, per_device(): lax.all_to_all(outgoing, ('rows', 'table'), split_axis=0, concat_axis=0,...  20.9 us
    add x16, other arithmetic, place_one_block(): wanted = start + jnp.arange(block_rows, dtype=jnp.int32)  11 us
    dynamic_slice x16, local copies, waits for them, and re-layouts, place_requests(): return lax.map(place_one_block, starts).reshape(total)  10.7 us
  transfers between devices with their start and end apart: 2, of which 1 were waited for; matrix products, arithmetic and copies ran while one was open for 2% of the time, Pallas kernels for 0%

commit v1 on v0

v1 whole, which is shorter than its diff:
```python
import functools

import jax
import jax.numpy as jnp
from jax import lax
from jax.experimental import pallas as pl
from jax.experimental.pallas import tpu as pltpu
from jax.sharding import PartitionSpec as P

CG_STEPS = 3
AXES = ("rows", "table")
VMEM_LIMIT = 48 * 2**20
NT = (((1,), (1,)), ((), ()))


def place_kernel(slots_ref, rows_ref, out_ref):
    users, links = slots_ref.shape
    devices, capacity = out_ref.shape
    owner_id = lax.broadcasted_iota(jnp.int32, (devices, links), 0)
    lane_id = lax.broadcasted_iota(jnp.int32, (2 * capacity, links), 0)
    upper = lane_id < capacity
    slot_id = jnp.where(upper, lane_id, lane_id - capacity)
    total = jnp.zeros((devices, 2 * capacity), jnp.float32)
    for user in range(0, users, 2):
        owners, named = [], []
        for one in (user, user + 1):
            slots = slots_ref[one : one + 1, :]
            rows = rows_ref[one : one + 1, :]
            owner = slots // capacity
            place = slots - owner * capacity
            high = (rows // 128).astype(jnp.float32)
            low = (rows % 128).astype(jnp.float32)
            owners.append(jnp.where(owner_id == owner, 1.0, 0.0).astype(jnp.bfloat16))
            value = jnp.where(upper, high, low)
            named.append(jnp.where(slot_id == place, value, 0.0).astype(jnp.bfloat16))
        total = total + lax.dot_general(
            jnp.concatenate(owners, axis=1),
            jnp.concatenate(named, axis=1),
            NT,
            preferred_element_type=jnp.float32,
        )
    high, low = total[:, :capacity], total[:, capacity:]
    out_ref[...] = (high * 128.0 + low).astype(jnp.int32)


def place_requests(link_slots, link_rows, devices, capacity):
    return pl.pallas_call(
        place_kernel,
        out_shape=jax.ShapeDtypeStruct((devices, capacity), jnp.int32),
        in_specs=[pl.BlockSpec(memory_space=pltpu.VMEM)] * 2,
        out_specs=pl.BlockSpec(memory_space=pltpu.VMEM),
        compiler_params=pltpu.CompilerParams(vmem_limit_bytes=VMEM_LIMIT),
        cost_estimate=pl.CostEstimate(flops=2 * 8192 * 128 * 128, bytes_accessed=98304, transcendentals=0),
    )(link_slots, link_rows)


def widen(source_ref, wide_ref, step):
    def one(block, carry):
        start = pl.multiple_of(block * step, step)
        wide_ref[pl.ds(start, step), :] = source_ref[pl.ds(start, step), :].astype(jnp.float32)
        return carry

    lax.fori_loop(0, source_ref.shape[0] // step, one, 0)


def fetch_kernel(index_ref, table_ref, out_ref, wide_ref):
    devices, capacity = index_ref.shape
    widen(table_ref, wide_ref, 256)

    def one(device, carry):
        rows = [wide_ref[pl.ds(index_ref[device, slot], 1), :] for slot in range(capacity)]
        out_ref[device] = jnp.concatenate(rows, axis=0).astype(jnp.bfloat16)
        return carry

    lax.fori_loop(0, devices, one, 0)


def fetch_rows(asked, item_table):
    devices, capacity = asked.shape
    items, features = item_table.shape
    return pl.pallas_call(
        fetch_kernel,
        out_shape=jax.ShapeDtypeStruct((devices, capacity, features), jnp.bfloat16),
        in_specs=[pl.BlockSpec(memory_space=pltpu.SMEM), pl.BlockSpec(memory_space=pltpu.VMEM)],
        out_specs=pl.BlockSpec(memory_space=pltpu.VMEM),
        scratch_shapes=[pltpu.VMEM((items, features), jnp.float32)],
        compiler_params=pltpu.CompilerParams(vmem_limit_bytes=VMEM_LIMIT),
        cost_estimate=pl.CostEstimate(flops=0, bytes_accessed=24 * 2**20, transcendentals=0),
    )(asked, item_table)


def split(value):
    high = value.astype(jnp.bfloat16)
    low = (value - high.astype(jnp.float32)).astype(jnp.bfloat16)
    return high, low


def solve_kernel(
    slots_ref, arrived_ref, weights_ref, counts_ref, start_ref, shared_ref, out_ref, wide_ref, conf_ref, system_ref
):
    users, links = slots_ref.shape
    features = arrived_ref.shape[1]
    widen(arrived_ref, wide_ref, 256)
    link_id = lax.broadcasted_iota(jnp.int32, (users, links), 1)
    conf_ref[...] = jnp.where(
        link_id < counts_ref[...], 1.0 + weights_ref[...].astype(jnp.float32) / 8.0, 0.0
    )
    user_lane = lax.broadcasted_iota(jnp.int32, (features, 2 * users), 1)
    user_lane = jnp.where(user_lane < users, user_lane, user_lane - users)
    ones = jnp.ones((links, features), jnp.bfloat16)

    def form(user, target):
        rows = [wide_ref[pl.ds(slots_ref[user, link], 1), :] for link in range(links)]
        fetched = jnp.concatenate(rows, axis=0)
        scaled = (fetched.T * conf_ref[pl.ds(user, 1), :]).astype(jnp.bfloat16)
        both = jnp.dot(
            scaled,
            jnp.concatenate([fetched.astype(jnp.bfloat16), ones], axis=1),
            preferred_element_type=jnp.float32,
        )
        high, low = split(both[:, :features])
        start = pl.multiple_of(user * features, features)
        system_ref[pl.ds(start, features), :features] = high
        system_ref[pl.ds(start, features), features:] = low
        return jnp.where(user_lane == user, both[:, features:], target)

    target = lax.fori_loop(0, users, form, jnp.zeros((features, 2 * users), jnp.float32))
    shared = jnp.concatenate(split(shared_ref[...]), axis=1)
    first_half = lax.broadcasted_iota(jnp.int32, (features, 2 * users), 1) < users
    together = 4

    def apply_system(vector):
        high, low = split(vector)
        half = jnp.where(first_half, high.astype(jnp.float32), low.astype(jnp.float32)).astype(jnp.bfloat16)
        operand = jnp.concatenate([half, half], axis=0)

        def some(block, image):
            start = pl.multiple_of(block * together * features, together * features)
            product = jnp.dot(
                system_ref[pl.ds(start, together * features), :], operand, preferred_element_type=jnp.float32
            )
            for one in range(together):
                piece = product[one * features : (one + 1) * features]
                image = jnp.where(user_lane == block * together + one, piece, image)
            return image

        image = lax.fori_loop(0, users // together, some, jnp.zeros((features, 2 * users), jnp.float32))
        image = image + jnp.dot(shared, operand, preferred_element_type=jnp.float32)
        return image + pltpu.roll(image, users, 1)

    start_rows = start_ref[...]
    estimate = jnp.concatenate([start_rows, start_rows], axis=0).T
    residual = target - apply_system(estimate)
    direction = residual
    norm_now = jnp.sum(residual * residual, axis=0, keepdims=True)
    for _ in range(CG_STEPS):
        image = apply_system(direction)
        curvature = jnp.sum(direction * image, axis=0, keepdims=True)
        step_len = norm_now / (curvature + 1e-06)
        estimate = estimate + step_len * direction
        residual = residual - step_len * image
        norm_next = jnp.sum(residual * residual, axis=0, keepdims=True)
        direction = residual + norm_next / (norm_now + 1e-06) * direction
        norm_now = norm_next
    out_ref[...] = estimate.T[:users]


def solve_rows(link_slots, arrived, link_weights, link_counts, user_rows, shared):
    users, links = link_slots.shape
    features = user_rows.shape[1]
    vmem = pl.BlockSpec(memory_space=pltpu.VMEM)
    return pl.pallas_call(
        solve_kernel,
        out_shape=jax.ShapeDtypeStruct((users, features), jnp.float32),
        in_specs=[pl.BlockSpec(memory_space=pltpu.SMEM)] + [vmem] * 5,
        out_specs=vmem,
        scratch_shapes=[
            pltpu.VMEM(arrived.shape, jnp.float32),
            pltpu.VMEM((users, links), jnp.float32),
            pltpu.VMEM((users * features, 2 * features), jnp.bfloat16),
        ],
        compiler_params=pltpu.CompilerParams(vmem_limit_bytes=VMEM_LIMIT),
        cost_estimate=pl.CostEstimate(flops=2**32, bytes_accessed=24 * 2**20, transcendentals=0),
    )(link_slots, arrived, link_weights, link_counts.reshape(users, 1), user_rows, shared)


def exchange(value):
    return lax.all_to_all(value, AXES, split_axis=0, concat_axis=0, tiled=True)


def per_device(item_table, user_rows, link_rows, link_slots, link_weights, link_counts):
    users, features = user_rows.shape
    links = link_rows.shape[1]
    devices = lax.axis_size("rows") * lax.axis_size("table")
    capacity = users * links // devices
    total_items = item_table.shape[0] * devices
    asked = exchange(place_requests(link_slots, link_rows, devices, capacity))
    arrived = exchange(fetch_rows(asked, item_table)).reshape(users * links, features)
    partial = jnp.dot(item_table.T, item_table, preferred_element_type=jnp.float32)
    own_row = jnp.sum(exchange(partial), axis=0, keepdims=True)
    gramian = exchange(jnp.broadcast_to(own_row, (features, features)))
    shared = gramian * (links / total_items) + 0.5 * links * jnp.eye(features, dtype=jnp.float32)
    return solve_rows(link_slots, arrived, link_weights, link_counts, user_rows, shared)


def solution(mesh):
    placed = (P(AXES, None),) * 5 + (P(AXES),)
    return jax.shard_map(
        per_device,
        mesh=mesh,
        in_specs=placed,
        out_specs=P(AXES, None),
        check_vma=False,
    )
```

time: 393 us -> 135 us (0.34)
  matrix products: 145 us -> 5.39 us
  waiting for transfers between devices: 145 us -> 47.7 us
  Pallas kernels: 0 us -> 50.4 us
  local copies, waits for them, and re-layouts: 46.1 us -> 0.79 us
  starting transfers between devices: 4.43 us -> 30 us
  blocking collectives: 20.9 us -> 0 us
  other arithmetic: 16 us -> 0.17 us
  between operations: 13.6 us -> 0.09 us
    psum x1 -> x0, waiting for transfers between devices: 145 us -> none  [per_device(): gramian = lax.psum(partial_value, ('rows', 'table'))]
    dot_general x37 -> x0, matrix products: 139 us -> none  [the longest x16 56.3 us: order_one_block(): jnp.dot(selector, arrived, preferred_element_type=jnp.float32)]
    pallas_call x0 -> x3, Pallas kernels: none -> 50.4 us  [the longest x1 37 us: solve_rows(): pl.pallas_call(solve_kernel, out_shape=jax.ShapeDtypeStruct((users, featu...]
    all_to_all x1 -> x4, waiting for transfers between devices: 0.01 us -> 47.7 us  [exchange(): return lax.all_to_all(value, AXES, split_axis=0, concat_axis=0, tiled=True)]
    gather x1 -> x0, local copies, waits for them, and re-layouts: 30.7 us -> none  [per_device(): item_table[lax.all_to_all(outgoing, ('rows', 'table'), split_axis=0, conc...]
    all_to_all x1 -> x4, starting transfers between devices: 4.39 us -> 30 us  [exchange(): return lax.all_to_all(value, AXES, split_axis=0, concat_axis=0, tiled=True)]
    all_to_all x1 -> x0, blocking collectives: 20.9 us -> none  [per_device(): lax.all_to_all(outgoing, ('rows', 'table'), split_axis=0, concat_axis=0,...]
    add x36 -> x1, other arithmetic: 12.9 us -> 0.01 us  [per_device(): gramian * (links / total_items)]
  transfers between devices with their start and end apart: 2 -> 4, of which waited for: 1 -> 3; matrix products, arithmetic and copies ran while one was open for 2% -> 0% of each run, Pallas kernels for 0% -> 10%
where the time goes in v1:
time: 135 us
  Pallas kernels  50.4 us (37%)
  waiting for transfers between devices  47.7 us (35%)
  starting transfers between devices  30 us (22%)
  matrix products  5.39 us (4%)
    all_to_all x4, waiting for transfers between devices, exchange(): return lax.all_to_all(value, AXES, split_axis=0, concat_axis=0, tiled=True)  47.7 us
    pallas_call x1, Pallas kernels, solve_rows(): pl.pallas_call(solve_kernel, out_shape=jax.ShapeDtypeStruct((users, featu...  37 us
    all_to_all x4, starting transfers between devices, exchange(): return lax.all_to_all(value, AXES, split_axis=0, concat_axis=0, tiled=True)  30 us
    pallas_call x1, Pallas kernels, fetch_rows(): pl.pallas_call(fetch_kernel, out_shape=jax.ShapeDtypeStruct((devices, cap...  11.6 us
    dot_general x1, matrix products, per_device(): jnp.dot(item_table.T, item_table, preferred_element_type=jnp.float32)  5.39 us
  transfers between devices with their start and end apart: 4, of which 3 were waited for; matrix products, arithmetic and copies ran while one was open for 0% of the time, Pallas kernels for 10%

profile of v1, /device:TPU:1, one launch (start us, length us, event | category | flops | bytes accessed | tf_op | source)
XLA Modules:
  0.0 134.5 jit_solution(11253256761013849249)
XLA Ops:
  0.0 0.0 copy-start
  0.0 5.4 %fusion = f32[128,128]{1,0:T(8,128)} fusion(bf16[16384,128]{1,0:T(8,128)(2,1)} %table_ref.1), kind=kOutput, calls=%fused_computation.2 | convolution fusion | flops 536870912 | bytes 4259840 | tf_op jit(solution)/shard_map/dot_general | solution.py:199
  5.4 11.5 %all-to-all-start.2 = ((f32[128,1,128]{2,1,0:T(1,128)}), f32[128,1,128]{2,1,0:T(1,128)S(1)}, u32[]{:S(2)}, u32[]{:S(2)}) async-start(f32[128,1,128]{2,1,0:T(1,128)} %bitcast.6), calls=%async_computation.2 | async-start | bytes 131072 | tf_op jit(solution)/shard_map/all_to_all | solution.py:188
  16.9 0.0 copy-done
  16.9 0.0 copy-done.1
  16.9 1.8 %shard_map.64 = s32[128,64]{1,0:T(8,128)} custom-call(s32[64,128]{1,0:T(8,128)S(1)} %copy-done.1, s32[64,128]{1,0:T(8,128)S(1)} %copy-done), custom_call_target="tpu_custom_call" | custom-call | flops 268435456 | bytes 98304 | tf_op jit(solution)/shard_map/pallas_call | solution.py:47
  18.7 7.8 %all-to-all-done.2 = f32[128,1,128]{2,1,0:T(1,128)S(1)} async-done(((f32[128,1,128]{2,1,0:T(1,128)}), f32[128,1,128]{2,1,0:T(1,128)S(1)}, u32[]{:S(2)}, u32[]{:S(2)}) %all-to-all-start.2) | async-done | bytes 65568 | tf_op jit(solution)/shard_map/all_to_all | solution.py:188
  26.5 4.4 %all-to-all-start = ((s32[128,1,64]{2,1,0:T(1,128)}), s32[128,1,64]{2,1,0:T(1,128)S(1)}, u32[]{:S(2)}, u32[]{:S(2)}) async-start(s32[128,1,64]{2,1,0:T(1,128)} %bitcast.1), calls=%async_computation | async-start | bytes 131072 | tf_op jit(solution)/shard_map/all_to_all | solution.py:188
  30.9 0.2 reduce_sum.9
  31.0 9.5 %all-to-all-done = s32[128,1,64]{2,1,0:T(1,128)S(1)} async-done(((s32[128,1,64]{2,1,0:T(1,128)}), s32[128,1,64]{2,1,0:T(1,128)S(1)}, u32[]{:S(2)}, u32[]{:S(2)}) %all-to-all-start) | async-done | bytes 32800 | tf_op jit(solution)/shard_map/all_to_all | solution.py:188
  40.5 0.7 broadcast_in_dim.2
  41.2 4.4 %all-to-all-start.3 = ((f32[128,1,128]{2,1,0:T(1,128)}), f32[128,1,128]{2,1,0:T(1,128)S(1)}, u32[]{:S(2)}, u32[]{:S(2)}) async-start(f32[128,1,128]{2,1,0:T(1,128)} %broadcast_in_dim.2), calls=%async_computation.3 | async-start | bytes 131072 | tf_op jit(solution)/shard_map/all_to_all | solution.py:188
  45.6 0.0 copy-start.4
  45.6 0.0 copy-start.2
  45.6 0.0 copy-start.3
  45.6 11.6 %shard_map.65 = bf16[128,64,128]{2,1,0:T(8,128)(2,1)} custom-call(s32[128,64]{1,0:T(8,128)S(1)} %bitcast.15, bf16[16384,128]{1,0:T(8,128)(2,1)} %table_ref.1), custom_call_target="tpu_custom_call" | custom-call | bytes 25165824 | tf_op jit(solution)/shard_map/pallas_call | solution.py:81
  57.2 0.0 all-to-all-done.3
  57.2 9.8 %all-to-all-start.1 = ((bf16[128,64,128]{2,1,0:T(8,128)(2,1)}), bf16[128,64,128]{2,1,0:T(8,128)(2,1)S(1)}, u32[]{:S(2)}, u32[]{:S(2)}) async-start(bf16[128,64,128]{2,1,0:T(8,128)(2,1)} %shard_map.65), calls=%async_computation.1 | async-start | bytes 4194304 | tf_op jit(solution)/shard_map/all_to_all | solution.py:188
  67.0 0.0 copy-done.4
  67.0 0.1 copy.11.counts_ref
  67.1 30.4 %all-to-all-done.1 = bf16[128,64,128]{2,1,0:T(8,128)(2,1)S(1)} async-done(((bf16[128,64,128]{2,1,0:T(8,128)(2,1)}), bf16[128,64,128]{2,1,0:T(8,128)(2,1)S(1)}, u32[]{:S(2)}, u32[]{:S(2)}) %all-to-all-start.1) | async-done | bytes 2097184 | tf_op jit(solution)/shard_map/all_to_all | solution.py:188
  97.5 0.0 copy-done.2
  97.5 0.0 copy-done.3
  97.5 37.0 %shard_map.66 = f32[64,128]{1,0:T(8,128)} custom-call(s32[64,128]{1,0:T(8,128)S(1)} %copy-done.1, bf16[8192,128]{1,0:T(8,128)(2,1)S(1)} %bitcast.14, s32[64,128]{1,0:T(8,128)S(1)} %copy-done.2, s32[64,1]{1,0:T(8,128)S(1)} %copy.11.counts_ref, f32[64,128]{1,0:T(8,128)S(1)} %copy-done.3, f32[128,128]{1,0:T(8,128)S(1)} %bitcast_add_fusion.shared_ref), custom_call_target="tpu_custom_call" | custom-call | flops 4294967296 | bytes 25165824 | tf_op jit(solution)/shard_map/pallas_call | solution.py:172
  (2 shorter events, 0.0 us)
Async XLA Ops:
  0.0 16.9 %copy-start = (s32[64,128]{1,0:T(8,128)S(1)}, s32[64,128]{1,0:T(8,128)}, u32[]{:S(2)}) copy-start(s32[64,128]{1,0:T(8,128)} %rows_ref.1) | copy-start | bytes 98308
  0.0 16.9 %copy-start.1 = (s32[64,128]{1,0:T(8,128)S(1)}, s32[64,128]{1,0:T(8,128)}, u32[]{:S(2)}) copy-start(s32[64,128]{1,0:T(8,128)} %slots_ref.3) | copy-start | bytes 98308
  5.4 21.1 %all-to-all-start.2 = ((f32[128,1,128]{2,1,0:T(1,128)}), f32[128,1,128]{2,1,0:T(1,128)S(1)}, u32[]{:S(2)}, u32[]{:S(2)}) async-start(f32[128,1,128]{2,1,0:T(1,128)} %bitcast.6), calls=%async_computation.2 | async-start | bytes 131072 | tf_op jit(solution)/shard_map/all_to_all | solution.py:188
  26.5 14.0 %all-to-all-start = ((s32[128,1,64]{2,1,0:T(1,128)}), s32[128,1,64]{2,1,0:T(1,128)S(1)}, u32[]{:S(2)}, u32[]{:S(2)}) async-start(s32[128,1,64]{2,1,0:T(1,128)} %bitcast.1), calls=%async_computation | async-start | bytes 131072 | tf_op jit(solution)/shard_map/all_to_all | solution.py:188
  41.2 16.1 %all-to-all-start.3 = ((f32[128,1,128]{2,1,0:T(1,128)}), f32[128,1,128]{2,1,0:T(1,128)S(1)}, u32[]{:S(2)}, u32[]{:S(2)}) async-start(f32[128,1,128]{2,1,0:T(1,128)} %broadcast_in_dim.2), calls=%async_computation.3 | async-start | bytes 131072 | tf_op jit(solution)/shard_map/all_to_all | solution.py:188
  45.6 21.4 %copy-start.4 = (s32[64]{0:T(128)S(1)}, s32[64]{0:T(128)}, u32[]{:S(2)}) copy-start(s32[64]{0:T(128)} %param.11) | copy-start | bytes 772
  45.6 51.9 %copy-start.2 = (s32[64,128]{1,0:T(8,128)S(1)}, s32[64,128]{1,0:T(8,128)}, u32[]{:S(2)}) copy-start(s32[64,128]{1,0:T(8,128)} %weights_ref.1) | copy-start | bytes 98308
  45.6 51.9 %copy-start.3 = (f32[64,128]{1,0:T(8,128)S(1)}, f32[64,128]{1,0:T(8,128)}, u32[]{:S(2)}) copy-start(f32[64,128]{1,0:T(8,128)} %start_ref.1) | copy-start | bytes 98308
  57.2 40.3 %all-to-all-start.1 = ((bf16[128,64,128]{2,1,0:T(8,128)(2,1)}), bf16[128,64,128]{2,1,0:T(8,128)(2,1)S(1)}, u32[]{:S(2)}, u32[]{:S(2)}) async-start(bf16[128,64,128]{2,1,0:T(8,128)(2,1)} %shard_map.65), calls=%async_computation.1 | async-start | bytes 4194304 | tf_op jit(solution)/shard_map/all_to_all | solution.py:188

commit v2 on v1

v2 whole, which is shorter than its diff:
```python
import functools

import jax
import jax.numpy as jnp
from jax import lax
from jax.experimental import pallas as pl
from jax.experimental.pallas import tpu as pltpu
from jax.sharding import PartitionSpec as P

CG_STEPS = 3
BATCH = 32
TOGETHER = 8
AXES = ("rows", "table")
VMEM_LIMIT = 60 * 2**20
NT = (((1,), (1,)), ((), ()))
TN = (((0,), (0,)), ((), ()))
TABLE_STEP = 2048
FETCH_UNROLL = 4
TAIL = 8


def ask_kernel(slots_hbm, rows_hbm, table_hbm, out_ref, slots_ref, rows_ref, table_ref, sems):
    copies = [
        pltpu.make_async_copy(source, target, sems.at[at])
        for at, (source, target) in enumerate(
            ((slots_hbm, slots_ref), (rows_hbm, rows_ref), (table_hbm, table_ref))
        )
    ]
    for copy in copies:
        copy.start()
    users, links = slots_ref.shape
    devices = out_ref.shape[0]
    items, features = table_ref.shape
    capacity = users * links // devices
    owner_id = lax.broadcasted_iota(jnp.int32, (devices, links), 0)
    lane_id = lax.broadcasted_iota(jnp.int32, (2 * capacity, links), 0)
    upper = lane_id < capacity
    slot_id = jnp.where(upper, lane_id, lane_id - capacity)
    copies[0].wait()
    copies[1].wait()
    total = jnp.zeros((devices, 2 * capacity), jnp.float32)
    for user in range(0, users, 2):
        owners, named = [], []
        for one in (user, user + 1):
            slots = slots_ref[one : one + 1, :]
            rows = rows_ref[one : one + 1, :]
            owner = slots // capacity
            place = slots - owner * capacity
            high = (rows // 128).astype(jnp.float32)
            low = (rows % 128).astype(jnp.float32)
            owners.append(jnp.where(owner_id == owner, 1.0, 0.0).astype(jnp.bfloat16))
            value = jnp.where(upper, high, low)
            named.append(jnp.where(slot_id == place, value, 0.0).astype(jnp.bfloat16))
        total = total + lax.dot_general(
            jnp.concatenate(owners, axis=1),
            jnp.concatenate(named, axis=1),
            NT,
            preferred_element_type=jnp.float32,
        )
    asked = total * 128.0 + pltpu.roll(total, capacity, 1)
    lane = lax.broadcasted_iota(jnp.int32, asked.shape, 1)
    out_ref[:, : 2 * capacity] = jnp.where(lane < capacity, asked, 0.0)
    copies[2].wait()
    gramian = jnp.zeros((features, features), jnp.float32)
    for start in range(0, items, TABLE_STEP):
        block = table_ref[start : start + TABLE_STEP, :]
        gramian = gramian + lax.dot_general(block, block, TN, preferred_element_type=jnp.float32)
    out_ref[:, 2 * capacity :] = gramian


def ask(link_slots, link_rows, item_table, devices):
    users, links = link_slots.shape
    features = item_table.shape[1]
    capacity = users * links // devices
    return pl.pallas_call(
        ask_kernel,
        out_shape=jax.ShapeDtypeStruct((devices, 2 * capacity + features), jnp.float32),
        in_specs=[pl.BlockSpec(memory_space=pl.ANY)] * 3,
        out_specs=pl.BlockSpec(memory_space=pltpu.VMEM),
        scratch_shapes=[
            pltpu.VMEM(link_slots.shape, jnp.int32),
            pltpu.VMEM(link_rows.shape, jnp.int32),
            pltpu.VMEM(item_table.shape, jnp.bfloat16),
            pltpu.SemaphoreType.DMA((3,)),
        ],
        compiler_params=pltpu.CompilerParams(vmem_limit_bytes=VMEM_LIMIT),
        cost_estimate=pl.CostEstimate(flops=2**30, bytes_accessed=2**22, transcendentals=0),
    )(link_slots, link_rows, item_table)


def fetch_kernel(received_ref, table_hbm, out_ref, table_ref, wide_ref, index_vmem, index_ref, table_sems, index_sem):
    items, features = table_ref.shape
    devices, held, _ = out_ref.shape
    capacity = held - TAIL
    parts = items // TABLE_STEP
    copies = []
    for part in range(parts):
        span = pl.ds(part * TABLE_STEP, TABLE_STEP)
        copies.append(pltpu.make_async_copy(table_hbm.at[span], table_ref.at[span], table_sems.at[part]))
        copies[-1].start()
    index_vmem[...] = received_ref[:, : 2 * capacity].astype(jnp.int32)
    index_copy = pltpu.make_async_copy(index_vmem, index_ref, index_sem)
    index_copy.start()
    row = jnp.sum(received_ref[:, 2 * capacity :], axis=0, keepdims=True)
    high, rest = split(row)
    low, _ = split(row - high.astype(jnp.float32) - rest.astype(jnp.float32))
    terms = [high.astype(jnp.float32), rest.astype(jnp.float32), low.astype(jnp.float32)]
    tail = jnp.concatenate(terms + [jnp.zeros((TAIL - 3, features), jnp.float32)], axis=0).astype(jnp.bfloat16)
    for part, copy in enumerate(copies):
        copy.wait()
        for start in range(part * TABLE_STEP, (part + 1) * TABLE_STEP, 256):
            wide_ref[start : start + 256, :] = table_ref[start : start + 256, :].astype(jnp.float32)
    index_copy.wait()

    def one(device, carry):
        rows = [wide_ref[pl.ds(index_ref[device, slot], 1), :] for slot in range(capacity)]
        out_ref[device, :capacity, :] = jnp.concatenate(rows, axis=0).astype(jnp.bfloat16)
        out_ref[device, capacity:, :] = tail
        return carry

    lax.fori_loop(0, devices, one, 0, unroll=FETCH_UNROLL)


def fetch_rows(received, item_table, capacity):
    devices = received.shape[0]
    items, features = item_table.shape
    vmem = pl.BlockSpec(memory_space=pltpu.VMEM)
    return pl.pallas_call(
        fetch_kernel,
        out_shape=jax.ShapeDtypeStruct((devices, capacity + TAIL, features), jnp.bfloat16),
        in_specs=[vmem, pl.BlockSpec(memory_space=pl.ANY)],
        out_specs=vmem,
        scratch_shapes=[
            pltpu.VMEM((items, features), jnp.bfloat16),
            pltpu.VMEM((items, features), jnp.float32),
            pltpu.VMEM((devices, 2 * capacity), jnp.int32),
            pltpu.SMEM((devices, 2 * capacity), jnp.int32),
            pltpu.SemaphoreType.DMA((items // TABLE_STEP,)),
            pltpu.SemaphoreType.DMA,
        ],
        compiler_params=pltpu.CompilerParams(vmem_limit_bytes=VMEM_LIMIT),
        cost_estimate=pl.CostEstimate(flops=0, bytes_accessed=24 * 2**20, transcendentals=0),
    )(received, item_table)


def split(value):
    high = value.astype(jnp.bfloat16)
    low = (value - high.astype(jnp.float32)).astype(jnp.bfloat16)
    return high, low


def solve_kernel(
    total_items, slots_ref, arrived_ref, weights_ref, counts_ref, start_ref, out_ref, wide_ref, shared_ref, conf_ref, system_ref
):
    users, links = slots_ref.shape
    devices, held, features = arrived_ref.shape
    capacity = held - TAIL

    def widen(device, carry):
        start = pl.multiple_of(device * capacity, capacity)
        wide_ref[pl.ds(start, capacity), :] = arrived_ref[device, :capacity, :].astype(jnp.float32)
        tail = arrived_ref[device, capacity:, :].astype(jnp.float32)
        shared_ref[pl.ds(device, 1), :] = jnp.sum(tail, axis=0, keepdims=True)
        return carry

    lax.fori_loop(0, devices, widen, 0, unroll=8)
    diagonal = jnp.where(
        lax.broadcasted_iota(jnp.int32, (features, features), 0)
        == lax.broadcasted_iota(jnp.int32, (features, features), 1),
        0.5 * links,
        0.0,
    )
    shared_ref[...] = shared_ref[...] * (links / total_items) + diagonal
    link_id = lax.broadcasted_iota(jnp.int32, (users, links), 1)
    conf_ref[...] = jnp.where(
        link_id < counts_ref[...], 1.0 + weights_ref[...].astype(jnp.float32) / 8.0, 0.0
    )
    lane = lax.broadcasted_iota(jnp.int32, (features, 2 * users), 1)
    user_lane = jnp.where(lane < users, lane, lane - users)
    ones = jnp.ones((links, 2 * users), jnp.bfloat16)

    def stationary(vector):
        high, low = split(vector)
        half = jnp.where(lane < users, high.astype(jnp.float32), low.astype(jnp.float32)).astype(jnp.bfloat16)
        return jnp.concatenate([half, half], axis=0)

    def both_halves(image):
        return image + pltpu.roll(image, users, 1)

    def form(user, operand, target, image):
        rows = [wide_ref[pl.ds(slots_ref[user, link], 1), :] for link in range(links)]
        fetched = jnp.concatenate(rows, axis=0)
        scaled = (fetched.T * conf_ref[user : user + 1, :]).astype(jnp.bfloat16)
        both = jnp.dot(
            scaled,
            jnp.concatenate([fetched.astype(jnp.bfloat16), ones], axis=1),
            preferred_element_type=jnp.float32,
        )
        system = jnp.concatenate(split(both[:, :features] + shared_ref[...]), axis=1)
        system_ref[user * features : (user + 1) * features, :] = system
        first = jnp.dot(system, operand, preferred_element_type=jnp.float32)
        mine = user_lane == user
        return jnp.where(mine, both[:, features:], target), jnp.where(mine, first, image)

    def apply_system(vector, first, last):
        operand = stationary(vector)
        image = jnp.zeros_like(vector)
        for user in range(first, last, TOGETHER):
            product = jnp.dot(
                system_ref[user * features : (user + TOGETHER) * features, :],
                operand,
                preferred_element_type=jnp.float32,
            )
            for one in range(TOGETHER):
                piece = product[one * features : (one + 1) * features]
                image = jnp.where(user_lane == user + one, piece, image)
        return both_halves(image)

    def refine(first, last, target, image, estimate):
        residual = target - both_halves(image)
        direction = residual
        norm_now = jnp.sum(residual * residual, axis=0, keepdims=True)
        for iteration in range(CG_STEPS):
            image = apply_system(direction, first, last)
            curvature = jnp.sum(direction * image, axis=0, keepdims=True)
            step_len = norm_now / (curvature + 1e-06)
            estimate = estimate + step_len * direction
            residual = residual - step_len * image
            norm_next = jnp.sum(residual * residual, axis=0, keepdims=True)
            direction = residual + norm_next / (norm_now + 1e-06) * direction
            norm_now = norm_next
        return estimate

    start_rows = start_ref[...]
    estimate = jnp.concatenate([start_rows, start_rows], axis=0).T
    operand = stationary(estimate)
    zero = jnp.zeros((features, 2 * users), jnp.float32)
    waiting = None
    for first in range(0, users, BATCH):
        target, image = zero, zero
        for user in range(first, first + BATCH):
            target, image = form(user, operand, target, image)
        if waiting is not None:
            estimate = refine(*waiting, estimate)
        waiting = (first, first + BATCH, target, image)
    out_ref[...] = refine(*waiting, estimate).T[:users]


def solve_rows(link_slots, arrived, link_weights, link_counts, user_rows, total_items):
    users, links = link_slots.shape
    features = user_rows.shape[1]
    vmem = pl.BlockSpec(memory_space=pltpu.VMEM)
    return pl.pallas_call(
        functools.partial(solve_kernel, total_items),
        out_shape=jax.ShapeDtypeStruct((users, features), jnp.float32),
        in_specs=[pl.BlockSpec(memory_space=pltpu.SMEM)] + [vmem] * 4,
        out_specs=vmem,
        scratch_shapes=[
            pltpu.VMEM((users * links, features), jnp.float32),
            pltpu.VMEM((features, features), jnp.float32),
            pltpu.VMEM((users, links), jnp.float32),
            pltpu.VMEM((users * features, 2 * features), jnp.bfloat16),
        ],
        compiler_params=pltpu.CompilerParams(vmem_limit_bytes=VMEM_LIMIT),
        cost_estimate=pl.CostEstimate(flops=2**32, bytes_accessed=24 * 2**20, transcendentals=0),
    )(link_slots, arrived, link_weights, link_counts.reshape(users, 1), user_rows)


def exchange(value):
    return lax.all_to_all(value, AXES, split_axis=0, concat_axis=0, tiled=True)


def per_device(item_table, user_rows, link_rows, link_slots, link_weights, link_counts):
    users, features = user_rows.shape
    links = link_rows.shape[1]
    devices = lax.axis_size("rows") * lax.axis_size("table")
    capacity = users * links // devices
    total_items = item_table.shape[0] * devices
    received = exchange(ask(link_slots, link_rows, item_table, devices))
    arrived = exchange(fetch_rows(received, item_table, capacity))
    return solve_rows(link_slots, arrived, link_weights, link_counts, user_rows, total_items)


def solution(mesh):
    placed = (P(AXES, None),) * 5 + (P(AXES),)
    return jax.shard_map(
        per_device,
        mesh=mesh,
        in_specs=placed,
        out_specs=P(AXES, None),
        check_vma=False,
    )
```

time: 135 us -> 91.8 us (0.68)
  starting transfers between devices: 30 us -> 4.22 us
  blocking collectives: 0 us -> 21.4 us
  Pallas kernels: 50.4 us -> 29.4 us
  waiting for transfers between devices: 47.7 us -> 32.6 us
  matrix products: 5.39 us -> 0 us
  local copies, waits for them, and re-layouts: 0.79 us -> 3.82 us
    all_to_all x4 -> x1, starting transfers between devices: 30 us -> 4.22 us  [exchange(): return lax.all_to_all(value, AXES, split_axis=0, concat_axis=0, tiled=True)]
    all_to_all x0 -> x1, blocking collectives: none -> 21.4 us  [exchange(): return lax.all_to_all(value, AXES, split_axis=0, concat_axis=0, tiled=True)]
    pallas_call x2, Pallas kernels: 38.8 us -> 18.1 us  [the longest x1 13.3 us: solve_rows(): pl.pallas_call(functools.partial(solve_kernel, total_items), out_shape=ja...]
    all_to_all x4 -> x1, waiting for transfers between devices: 47.7 us -> 32.6 us  [exchange(): return lax.all_to_all(value, AXES, split_axis=0, concat_axis=0, tiled=True)]
    dot_general x1 -> x0, matrix products: 5.39 us -> none  [per_device(): jnp.dot(item_table.T, item_table, preferred_element_type=jnp.float32)]
    unnamed x10 -> x5, local copies, waits for them, and re-layouts: 0.03 us -> 2.08 us
  transfers between devices with their start and end apart: 4 -> 1, of which waited for: 3 -> 1; matrix products, arithmetic and copies ran while one was open for 0% -> 1% of each run, Pallas kernels for 10% -> 0%
where the time goes in v2:
time: 91.8 us; the launch traced here: 91.5 us
  waiting for transfers between devices  32.6 us (36%)
  Pallas kernels  29.4 us (32%)
  blocking collectives  21.4 us (23%)
  starting transfers between devices  4.22 us (5%)
  local copies, waits for them, and re-layouts  3.82 us (4%)
    all_to_all x1, waiting for transfers between devices, exchange(): return lax.all_to_all(value, AXES, split_axis=0, concat_axis=0, tiled=True)  32.6 us
    all_to_all x1, blocking collectives, exchange(): return lax.all_to_all(value, AXES, split_axis=0, concat_axis=0, tiled=True)  21.4 us
    pallas_call x1, Pallas kernels, solve_rows(): pl.pallas_call(functools.partial(solve_kernel, total_items), out_shape=ja...  13.3 us
    pallas_call x1, Pallas kernels, fetch_rows(): pl.pallas_call(fetch_kernel, out_shape=jax.ShapeDtypeStruct((devices, cap...  11.3 us
    pallas_call x1, Pallas kernels, ask(): pl.pallas_call(ask_kernel, out_shape=jax.ShapeDtypeStruct((devices, 2 * c...  4.72 us
    all_to_all x1, starting transfers between devices, exchange(): return lax.all_to_all(value, AXES, split_axis=0, concat_axis=0, tiled=True)  4.22 us
    unnamed x5, local copies, waits for them, and re-layouts  2.08 us
  transfers between devices with their start and end apart: 1, of which 1 were waited for; matrix products, arithmetic and copies ran while one was open for 1% of the time, Pallas kernels for 0%

profile of v2, /device:TPU:1, one launch (start us, length us, event | category | flops | bytes accessed | tf_op | source)
XLA Modules:
  0.0 91.5 jit_solution(10443840169140340021)
XLA Ops:
  0.0 4.7 %shard_map.64 = f32[128,256]{1,0:T(8,128)} custom-call(s32[64,128]{1,0:T(8,128)} %slots_ref.1, s32[64,128]{1,0:T(8,128)} %rows_hbm.1, bf16[16384,128]{1,0:T(8,128)(2,1)} %table_hbm.3), custom_call_target="tpu_custom_call" | custom-call | flops 1073741824 | bytes 4194304 | tf_op jit(solution)/shard_map/pallas_call | solution.py:75
  4.7 1.0 %copy.8 = f32[128,1,256]{2,1,0:T(1,128)S(1)} copy(f32[128,1,256]{2,0,1:T(8,128)} %bitcast.6) | data formatting | bytes 262144 | tf_op jit(solution)/shard_map/all_to_all | solution.py:270
  5.8 21.4 %all_to_all.16 = f32[128,1,256]{2,1,0:T(1,128)S(1)} all-to-all(f32[128,1,256]{2,1,0:T(1,128)S(1)} %copy.8), channel_id=1, replica_groups=mesh['rows'=16,'table'=8] {'rows','table'}, dimensions={0} | all-to-all | bytes 262144 | tf_op jit(solution)/shard_map/all_to_all | solution.py:270
  27.2 0.7 copy.12
  27.9 11.3 %shard_map.65 = bf16[128,72,128]{2,1,0:T(8,128)(2,1)} custom-call(f32[128,256]{1,0:T(8,128)} %bitcast.5, bf16[16384,128]{1,0:T(8,128)(2,1)} %table_hbm.3), custom_call_target="tpu_custom_call" | custom-call | bytes 25165824 | tf_op jit(solution)/shard_map/pallas_call | solution.py:128
  39.2 0.0 copy-start.1
  39.2 4.2 %all-to-all-start.1 = ((bf16[128,72,128]{2,1,0:T(8,128)(2,1)}), bf16[128,72,128]{2,1,0:T(8,128)(2,1)S(1)}, u32[]{:S(2)}, u32[]{:S(2)}) async-start(bf16[128,72,128]{2,1,0:T(8,128)(2,1)} %shard_map.65), calls=%async_computation.1 | async-start | bytes 4718592 | tf_op jit(solution)/shard_map/all_to_all | solution.py:270
  43.4 0.0 copy-done.1
  43.5 0.7 copy.9.counts_ref
  44.2 32.6 %all-to-all-done.1.arrived_ref = bf16[128,72,128]{2,1,0:T(8,128)(2,1)S(1)} async-done(((bf16[128,72,128]{2,1,0:T(8,128)(2,1)}), bf16[128,72,128]{2,1,0:T(8,128)(2,1)S(1)}, u32[]{:S(2)}, u32[]{:S(2)}) %all-to-all-start.1) | async-done | bytes 2359328 | tf_op jit(solution)/shard_map/all_to_all | solution.py:270
  76.8 0.0 copy-start
  76.8 1.4 %copy-done = bf16[128,72,128]{2,1,0:T(8,128)(2,1)} copy-done((bf16[128,72,128]{2,1,0:T(8,128)(2,1)}, bf16[128,72,128]{2,1,0:T(8,128)(2,1)S(1)}, u32[]{:S(2)}) %copy-start) | copy-done | bytes 2359320
  78.2 13.3 %shard_map.66 = f32[64,128]{1,0:T(8,128)} custom-call(s32[64,128]{1,0:T(8,128)} %slots_ref.1, bf16[128,72,128]{2,1,0:T(8,128)(2,1)} %copy-done, s32[64,128]{1,0:T(8,128)} %weights_ref.1, s32[64,1]{1,0:T(8,128)} %copy.9.counts_ref, f32[64,128]{1,0:T(8,128)} %start_ref.1), custom_call_target="tpu_custom_call" | custom-call | flops 4294967296 | bytes 25165824 | tf_op jit(solution)/shard_map/pallas_call | solution.py:253
Async XLA Ops:
  39.2 4.2 %copy-start.1 = (s32[64]{0:T(128)S(1)}, s32[64]{0:T(128)}, u32[]{:S(2)}) copy-start(s32[64]{0:T(128)} %param.11) | copy-start | bytes 772
  39.2 37.5 %all-to-all-start.1 = ((bf16[128,72,128]{2,1,0:T(8,128)(2,1)}), bf16[128,72,128]{2,1,0:T(8,128)(2,1)S(1)}, u32[]{:S(2)}, u32[]{:S(2)}) async-start(bf16[128,72,128]{2,1,0:T(8,128)(2,1)} %shard_map.65), calls=%async_computation.1 | async-start | bytes 4718592 | tf_op jit(solution)/shard_map/all_to_all | solution.py:270
  76.8 1.4 %copy-start = (bf16[128,72,128]{2,1,0:T(8,128)(2,1)}, bf16[128,72,128]{2,1,0:T(8,128)(2,1)S(1)}, u32[]{:S(2)}) copy-start(bf16[128,72,128]{2,1,0:T(8,128)(2,1)S(1)} %all-to-all-done.1.arrived_ref) | copy-start | bytes 7077892

commit v3 on v2

--- a/solution.py
+++ b/solution.py
@@ -8,22 +8,30 @@
 from jax.sharding import PartitionSpec as P
 
 CG_STEPS = 3
-BATCH = 32
-TOGETHER = 8
+BATCHES = (32, 32)
+TOGETHER = 4
 AXES = ("rows", "table")
 VMEM_LIMIT = 60 * 2**20
+SOLVE_LIMIT = 24 * 2**20
 NT = (((1,), (1,)), ((), ()))
 TN = (((0,), (0,)), ((), ()))
 TABLE_STEP = 2048
-FETCH_UNROLL = 4
+OUT_STEP = 16
+PLACE_FIRST = 32
 TAIL = 8
 
 
 def ask_kernel(slots_hbm, rows_hbm, table_hbm, out_ref, slots_ref, rows_ref, table_ref, sems):
+    half = table_ref.shape[0] // 2
     copies = [
         pltpu.make_async_copy(source, target, sems.at[at])
         for at, (source, target) in enumerate(
-            ((slots_hbm, slots_ref), (rows_hbm, rows_ref), (table_hbm, table_ref))
+            (
+                (slots_hbm, slots_ref),
+                (rows_hbm, rows_ref),
+                (table_hbm.at[pl.ds(0, half)], table_ref.at[pl.ds(0, half)]),
+                (table_hbm.at[pl.ds(half, half)], table_ref.at[pl.ds(half, half)]),
+            )
         )
     ]
     for copy in copies:
@@ -38,8 +46,8 @@
     slot_id = jnp.where(upper, lane_id, lane_id - capacity)
     copies[0].wait()
     copies[1].wait()
-    total = jnp.zeros((devices, 2 * capacity), jnp.float32)
-    for user in range(0, users, 2):
+
+    def place(user, total):
         owners, named = [], []
         for one in (user, user + 1):
             slots = slots_ref[one : one + 1, :]
@@ -51,21 +59,37 @@
             owners.append(jnp.where(owner_id == owner, 1.0, 0.0).astype(jnp.bfloat16))
             value = jnp.where(upper, high, low)
             named.append(jnp.where(slot_id == place, value, 0.0).astype(jnp.bfloat16))
-        total = total + lax.dot_general(
+        return total + lax.dot_general(
             jnp.concatenate(owners, axis=1),
             jnp.concatenate(named, axis=1),
             NT,
             preferred_element_type=jnp.float32,
         )
+
+    def add_items(start, gramian):
+        block = table_ref[start : start + TABLE_STEP, :]
+        return gramian + lax.dot_general(block, block, TN, preferred_element_type=jnp.float32)
+
+    total = jnp.zeros((devices, 2 * capacity), jnp.float32)
+    gramian = jnp.zeros((features, features), jnp.float32)
+    early = PLACE_FIRST
+    for user in range(0, early, 2):
+        total = place(user, total)
+    copies[2].wait()
+    starts = list(range(0, half, TABLE_STEP))
+    for user in range(early, users, 2):
+        total = place(user, total)
+        if starts and (user - early) % 8 == 0:
+            gramian = add_items(starts.pop(0), gramian)
+    for start in starts:
+        gramian = add_items(start, gramian)
     asked = total * 128.0 + pltpu.roll(total, capacity, 1)
     lane = lax.broadcasted_iota(jnp.int32, asked.shape, 1)
-    out_ref[:, : 2 * capacity] = jnp.where(lane < capacity, asked, 0.0)
-    copies[2].wait()
-    gramian = jnp.zeros((features, features), jnp.float32)
-    for start in range(0, items, TABLE_STEP):
-        block = table_ref[start : start + TABLE_STEP, :]
-        gramian = gramian + lax.dot_general(block, block, TN, preferred_element_type=jnp.float32)
-    out_ref[:, 2 * capacity :] = gramian
+    out_ref[:, 0, : 2 * capacity] = jnp.where(lane < capacity, asked, 0.0)
+    copies[3].wait()
+    for start in range(half, items, TABLE_STEP):
+        gramian = add_items(start, gramian)
+    out_ref[:, 0, 2 * capacity :] = gramian
 
 
 def ask(link_slots, link_rows, item_table, devices):
@@ -74,21 +98,23 @@
     capacity = users * links // devices
     return pl.pallas_call(
         ask_kernel,
-        out_shape=jax.ShapeDtypeStruct((devices, 2 * capacity + features), jnp.float32),
+        out_shape=jax.ShapeDtypeStruct((devices, 1, 2 * capacity + features), jnp.float32),
         in_specs=[pl.BlockSpec(memory_space=pl.ANY)] * 3,
         out_specs=pl.BlockSpec(memory_space=pltpu.VMEM),
         scratch_shapes=[
             pltpu.VMEM(link_slots.shape, jnp.int32),
             pltpu.VMEM(link_rows.shape, jnp.int32),
             pltpu.VMEM(item_table.shape, jnp.bfloat16),
-            pltpu.SemaphoreType.DMA((3,)),
+            pltpu.SemaphoreType.DMA((4,)),
         ],
         compiler_params=pltpu.CompilerParams(vmem_limit_bytes=VMEM_LIMIT),
         cost_estimate=pl.CostEstimate(flops=2**30, bytes_accessed=2**22, transcendentals=0),
     )(link_slots, link_rows, item_table)
 
 
-def fetch_kernel(received_ref, table_hbm, out_ref, table_ref, wide_ref, index_vmem, index_ref, table_sems, index_sem):
+def fetch_kernel(
+    received_ref, table_hbm, out_hbm, table_ref, wide_ref, index_vmem, index_ref, out_ref, table_sems, index_sem, out_sems
+):
     items, features = table_ref.shape
     devices, held, _ = out_ref.shape
     capacity = held - TAIL
@@ -98,10 +124,10 @@
         span = pl.ds(part * TABLE_STEP, TABLE_STEP)
         copies.append(pltpu.make_async_copy(table_hbm.at[span], table_ref.at[span], table_sems.at[part]))
         copies[-1].start()
-    index_vmem[...] = received_ref[:, : 2 * capacity].astype(jnp.int32)
+    index_vmem[...] = received_ref[:, 0, : 2 * capacity].astype(jnp.int32)
     index_copy = pltpu.make_async_copy(index_vmem, index_ref, index_sem)
     index_copy.start()
-    row = jnp.sum(received_ref[:, 2 * capacity :], axis=0, keepdims=True)
+    row = jnp.sum(received_ref[:, 0, 2 * capacity :], axis=0, keepdims=True)
     high, rest = split(row)
     low, _ = split(row - high.astype(jnp.float32) - rest.astype(jnp.float32))
     terms = [high.astype(jnp.float32), rest.astype(jnp.float32), low.astype(jnp.float32)]
@@ -112,13 +138,17 @@
             wide_ref[start : start + 256, :] = table_ref[start : start + 256, :].astype(jnp.float32)
     index_copy.wait()
 
-    def one(device, carry):
+    sent = []
+    for device in range(devices):
         rows = [wide_ref[pl.ds(index_ref[device, slot], 1), :] for slot in range(capacity)]
         out_ref[device, :capacity, :] = jnp.concatenate(rows, axis=0).astype(jnp.bfloat16)
         out_ref[device, capacity:, :] = tail
-        return carry
-
-    lax.fori_loop(0, devices, one, 0, unroll=FETCH_UNROLL)
+        if (device + 1) % OUT_STEP == 0:
+            span = pl.ds(device + 1 - OUT_STEP, OUT_STEP)
+            sent.append(pltpu.make_async_copy(out_ref.at[span], out_hbm.at[span], out_sems.at[len(sent)]))
+            sent[-1].start()
+    for copy in sent:
+        copy.wait()
 
 
 def fetch_rows(received, item_table, capacity):
@@ -129,14 +159,16 @@
         fetch_kernel,
         out_shape=jax.ShapeDtypeStruct((devices, capacity + TAIL, features), jnp.bfloat16),
         in_specs=[vmem, pl.BlockSpec(memory_space=pl.ANY)],
-        out_specs=vmem,
+        out_specs=pl.BlockSpec(memory_space=pl.ANY),
         scratch_shapes=[
             pltpu.VMEM((items, features), jnp.bfloat16),
             pltpu.VMEM((items, features), jnp.float32),
             pltpu.VMEM((devices, 2 * capacity), jnp.int32),
             pltpu.SMEM((devices, 2 * capacity), jnp.int32),
+            pltpu.VMEM((devices, capacity + TAIL, features), jnp.bfloat16),
             pltpu.SemaphoreType.DMA((items // TABLE_STEP,)),
             pltpu.SemaphoreType.DMA,
+            pltpu.SemaphoreType.DMA((devices // OUT_STEP,)),
         ],
         compiler_params=pltpu.CompilerParams(vmem_limit_bytes=VMEM_LIMIT),
         cost_estimate=pl.CostEstimate(flops=0, bytes_accessed=24 * 2**20, transcendentals=0),
@@ -202,26 +234,24 @@
         mine = user_lane == user
         return jnp.where(mine, both[:, features:], target), jnp.where(mine, first, image)
 
-    def apply_system(vector, first, last):
-        operand = stationary(vector)
-        image = jnp.zeros_like(vector)
-        for user in range(first, last, TOGETHER):
-            product = jnp.dot(
-                system_ref[user * features : (user + TOGETHER) * features, :],
-                operand,
-                preferred_element_type=jnp.float32,
-            )
-            for one in range(TOGETHER):
-                piece = product[one * features : (one + 1) * features]
-                image = jnp.where(user_lane == user + one, piece, image)
-        return both_halves(image)
-
     def refine(first, last, target, image, estimate):
         residual = target - both_halves(image)
         direction = residual
         norm_now = jnp.sum(residual * residual, axis=0, keepdims=True)
         for iteration in range(CG_STEPS):
-            image = apply_system(direction, first, last)
+            operand = stationary(direction)
+            image = jnp.zeros_like(direction)
+            for user in range(first, last, TOGETHER):
+                product = jnp.dot(
+                    system_ref[user * features : (user + TOGETHER) * features, :],
+                    operand,
+                    preferred_element_type=jnp.float32,
+                )
+                for one in range(TOGETHER):
+                    piece = product[one * features : (one + 1) * features]
+                    image = jnp.where(user_lane == user + one, piece, image)
+            yield None
+            image = both_halves(image)
             curvature = jnp.sum(direction * image, axis=0, keepdims=True)
             step_len = norm_now / (curvature + 1e-06)
             estimate = estimate + step_len * direction
@@ -229,21 +259,25 @@
             norm_next = jnp.sum(residual * residual, axis=0, keepdims=True)
             direction = residual + norm_next / (norm_now + 1e-06) * direction
             norm_now = norm_next
-        return estimate
+        yield estimate
 
     start_rows = start_ref[...]
     estimate = jnp.concatenate([start_rows, start_rows], axis=0).T
     operand = stationary(estimate)
     zero = jnp.zeros((features, 2 * users), jnp.float32)
-    waiting = None
-    for first in range(0, users, BATCH):
+    chains, last = [], 0
+    for batch in BATCHES:
+        first, last = last, last + batch
         target, image = zero, zero
-        for user in range(first, first + BATCH):
+        for user in range(first, last):
             target, image = form(user, operand, target, image)
-        if waiting is not None:
-            estimate = refine(*waiting, estimate)
-        waiting = (first, first + BATCH, target, image)
-    out_ref[...] = refine(*waiting, estimate).T[:users]
+        chains.append(refine(first, last, target, image, estimate if not chains else zero))
+    total = zero
+    for _ in range(CG_STEPS + 1):
+        done = [next(chain) for chain in chains]
+    for one in done:
+        total = total + one
+    out_ref[...] = total.T[:users]
 
 
 def solve_rows(link_slots, arrived, link_weights, link_counts, user_rows, total_items):
@@ -261,7 +295,7 @@
             pltpu.VMEM((users, links), jnp.float32),
             pltpu.VMEM((users * features, 2 * features), jnp.bfloat16),
         ],
-        compiler_params=pltpu.CompilerParams(vmem_limit_bytes=VMEM_LIMIT),
+        compiler_params=pltpu.CompilerParams(vmem_limit_bytes=SOLVE_LIMIT),
         cost_estimate=pl.CostEstimate(flops=2**32, bytes_accessed=24 * 2**20, transcendentals=0),
     )(link_slots, arrived, link_weights, link_counts.reshape(users, 1), user_rows)
 

time: 91.8 us -> 84 us (0.915)
  Pallas kernels: 29.4 us -> 24.2 us
  local copies, waits for them, and re-layouts: 3.82 us -> 0.12 us
    pallas_call x1, Pallas kernels: 11.3 us -> 8.35 us  [fetch_rows(): pl.pallas_call(fetch_kernel, out_shape=jax.ShapeDtypeStruct((devices, cap...]
    unnamed x5 -> x8, local copies, waits for them, and re-layouts: 2.08 us -> 0.03 us
    pallas_call x1, Pallas kernels: 13.3 us -> 11.5 us  [solve_rows(): pl.pallas_call(functools.partial(solve_kernel, total_items), out_shape=ja...]
    all_to_all x1 -> x0, local copies, waits for them, and re-layouts: 1.04 us -> none  [exchange(): return lax.all_to_all(value, AXES, split_axis=0, concat_axis=0, tiled=True)]
  transfers between devices with their start and end apart: 1 -> 1, of which waited for: 1 -> 1; matrix products, arithmetic and copies ran while one was open for 1% -> 0% of each run, Pallas kernels for 0% -> 0%
where the time goes in v3:
time: 84 us; the launch traced here: 83.7 us
  waiting for transfers between devices  33.2 us (40%)
  Pallas kernels  24.2 us (29%)
  blocking collectives  21.7 us (26%)
  starting transfers between devices  4.4 us (5%)
    all_to_all x1, waiting for transfers between devices, exchange(): return lax.all_to_all(value, AXES, split_axis=0, concat_axis=0, tiled=True)  33.2 us
    all_to_all x1, blocking collectives, exchange(): return lax.all_to_all(value, AXES, split_axis=0, concat_axis=0, tiled=True)  21.7 us
    pallas_call x1, Pallas kernels, solve_rows(): pl.pallas_call(functools.partial(solve_kernel, total_items), out_shape=ja...  11.5 us
    pallas_call x1, Pallas kernels, fetch_rows(): pl.pallas_call(fetch_kernel, out_shape=jax.ShapeDtypeStruct((devices, cap...  8.35 us
    all_to_all x1, starting transfers between devices, exchange(): return lax.all_to_all(value, AXES, split_axis=0, concat_axis=0, tiled=True)  4.4 us
    pallas_call x1, Pallas kernels, ask(): pl.pallas_call(ask_kernel, out_shape=jax.ShapeDtypeStruct((devices, 1, 2...  4.35 us
  transfers between devices with their start and end apart: 1, of which 1 were waited for; matrix products, arithmetic and copies ran while one was open for 0% of the time, Pallas kernels for 0%

profile of v3, /device:TPU:1, one launch (start us, length us, event | category | flops | bytes accessed | tf_op | source)
XLA Modules:
  0.0 83.7 jit_solution(3210976972773767112)
XLA Ops:
  0.0 4.3 %shard_map.64 = f32[128,1,256]{2,1,0:T(1,128)} custom-call(s32[64,128]{1,0:T(8,128)} %slots_ref.1, s32[64,128]{1,0:T(8,128)} %rows_hbm.1, bf16[16384,128]{1,0:T(8,128)(2,1)} %table_hbm.3), custom_call_target="tpu_custom_call" | custom-call | flops 1073741824 | bytes 4194304 | tf_op jit(solution)/shard_map/pallas_call | solution.py:99
  4.4 21.7 %all_to_all.10.received_ref = f32[128,1,256]{2,1,0:T(1,128)} all-to-all(f32[128,1,256]{2,1,0:T(1,128)} %shard_map.64), channel_id=1, replica_groups=mesh['rows'=16,'table'=8] {'rows','table'}, dimensions={0} | all-to-all | bytes 262144 | tf_op jit(solution)/shard_map/all_to_all | solution.py:304
  26.0 8.4 %shard_map.65 = bf16[128,72,128]{2,1,0:T(8,128)(2,1)} custom-call(f32[128,1,256]{2,1,0:T(1,128)} %all_to_all.10.received_ref, bf16[16384,128]{1,0:T(8,128)(2,1)} %table_hbm.3), custom_call_target="tpu_custom_call" | custom-call | bytes 25165824 | tf_op jit(solution)/shard_map/pallas_call | solution.py:158
  34.4 0.0 copy-start.3
  34.4 0.0 copy-start
  34.4 0.0 copy-start.1
  34.4 0.0 copy-start.2
  34.5 4.4 %all-to-all-start.1 = ((bf16[128,72,128]{2,1,0:T(8,128)(2,1)}), bf16[128,72,128]{2,1,0:T(8,128)(2,1)S(1)}, u32[]{:S(2)}, u32[]{:S(2)}) async-start(bf16[128,72,128]{2,1,0:T(8,128)(2,1)} %shard_map.65), calls=%async_computation.1 | async-start | bytes 4718592 | tf_op jit(solution)/shard_map/all_to_all | solution.py:304
  38.9 0.0 copy-done.3
  38.9 0.1 copy.7.counts_ref
  39.0 33.2 %all-to-all-done.1.arrived_ref = bf16[128,72,128]{2,1,0:T(8,128)(2,1)S(1)} async-done(((bf16[128,72,128]{2,1,0:T(8,128)(2,1)}), bf16[128,72,128]{2,1,0:T(8,128)(2,1)S(1)}, u32[]{:S(2)}, u32[]{:S(2)}) %all-to-all-start.1) | async-done | bytes 2359328 | tf_op jit(solution)/shard_map/all_to_all | solution.py:304
  72.2 0.0 copy-done
  72.2 0.0 copy-done.1
  72.2 0.0 copy-done.2
  72.2 11.5 %shard_map.66 = f32[64,128]{1,0:T(8,128)} custom-call(s32[64,128]{1,0:T(8,128)S(1)} %copy-done, bf16[128,72,128]{2,1,0:T(8,128)(2,1)S(1)} %all-to-all-done.1.arrived_ref, s32[64,128]{1,0:T(8,128)S(1)} %copy-done.1, s32[64,1]{1,0:T(8,128)S(1)} %copy.7.counts_ref, f32[64,128]{1,0:T(8,128)S(1)} %copy-done.2), custom_call_target="tpu_custom_call" | custom-call | flops 4294967296 | bytes 25165824 | tf_op jit(solution)/shard_map/pallas_call | solution.py:287
Async XLA Ops:
  34.4 4.5 %copy-start.3 = (s32[64]{0:T(128)S(1)}, s32[64]{0:T(128)}, u32[]{:S(2)}) copy-start(s32[64]{0:T(128)} %param.11) | copy-start | bytes 772
  34.4 37.7 %copy-start = (s32[64,128]{1,0:T(8,128)S(1)}, s32[64,128]{1,0:T(8,128)}, u32[]{:S(2)}) copy-start(s32[64,128]{1,0:T(8,128)} %slots_ref.1) | copy-start | bytes 98308
  34.4 37.7 %copy-start.1 = (s32[64,128]{1,0:T(8,128)S(1)}, s32[64,128]{1,0:T(8,128)}, u32[]{:S(2)}) copy-start(s32[64,128]{1,0:T(8,128)} %weights_ref.1) | copy-start | bytes 98308
  34.4 37.7 %copy-start.2 = (f32[64,128]{1,0:T(8,128)S(1)}, f32[64,128]{1,0:T(8,128)}, u32[]{:S(2)}) copy-start(f32[64,128]{1,0:T(8,128)} %start_ref.1) | copy-start | bytes 98308
  34.5 37.7 %all-to-all-start.1 = ((bf16[128,72,128]{2,1,0:T(8,128)(2,1)}), bf16[128,72,128]{2,1,0:T(8,128)(2,1)S(1)}, u32[]{:S(2)}, u32[]{:S(2)}) async-start(bf16[128,72,128]{2,1,0:T(8,128)(2,1)} %shard_map.65), calls=%async_computation.1 | async-start | bytes 4718592 | tf_op jit(solution)/shard_map/all_to_all | solution.py:304

commit v4 on v3

--- a/solution.py
+++ b/solution.py
@@ -11,12 +11,14 @@
 BATCHES = (32, 32)
 TOGETHER = 4
 AXES = ("rows", "table")
-VMEM_LIMIT = 60 * 2**20
+VMEM_LIMIT = 56 * 2**20
+FETCH_LIMIT = 24 * 2**20
 SOLVE_LIMIT = 24 * 2**20
 NT = (((1,), (1,)), ((), ()))
 TN = (((0,), (0,)), ((), ()))
 TABLE_STEP = 2048
-OUT_STEP = 16
+OUT_STEP = 8
+INDEX_PIECES = 4
 PLACE_FIRST = 32
 TAIL = 8
 
@@ -112,41 +114,40 @@
     )(link_slots, link_rows, item_table)
 
 
-def fetch_kernel(
-    received_ref, table_hbm, out_hbm, table_ref, wide_ref, index_vmem, index_ref, out_ref, table_sems, index_sem, out_sems
-):
+def fetch_kernel(received_ref, table_ref, out_hbm, wide_ref, index_vmem, index_ref, out_ref, index_sems, out_sems):
     items, features = table_ref.shape
     devices, held, _ = out_ref.shape
     capacity = held - TAIL
-    parts = items // TABLE_STEP
-    copies = []
-    for part in range(parts):
-        span = pl.ds(part * TABLE_STEP, TABLE_STEP)
-        copies.append(pltpu.make_async_copy(table_hbm.at[span], table_ref.at[span], table_sems.at[part]))
-        copies[-1].start()
-    index_vmem[...] = received_ref[:, 0, : 2 * capacity].astype(jnp.int32)
-    index_copy = pltpu.make_async_copy(index_vmem, index_ref, index_sem)
-    index_copy.start()
+    index = received_ref[:, 0, : 2 * capacity]
+    half = devices // 2
+    lane = lax.broadcasted_iota(jnp.int32, (half, 2 * capacity), 1)
+    index = jnp.where(lane < capacity, index[:half], pltpu.roll(index[half:], capacity, 1))
+    index_vmem[...] = index.astype(jnp.int32)
+    index_copies = []
+    for piece in range(INDEX_PIECES):
+        span = pl.ds(piece * (half // INDEX_PIECES), half // INDEX_PIECES)
+        index_copies.append(pltpu.make_async_copy(index_vmem.at[span], index_ref.at[span], index_sems.at[piece]))
+        index_copies[-1].start()
     row = jnp.sum(received_ref[:, 0, 2 * capacity :], axis=0, keepdims=True)
     high, rest = split(row)
     low, _ = split(row - high.astype(jnp.float32) - rest.astype(jnp.float32))
     terms = [high.astype(jnp.float32), rest.astype(jnp.float32), low.astype(jnp.float32)]
     tail = jnp.concatenate(terms + [jnp.zeros((TAIL - 3, features), jnp.float32)], axis=0).astype(jnp.bfloat16)
-    for part, copy in enumerate(copies):
-        copy.wait()
-        for start in range(part * TABLE_STEP, (part + 1) * TABLE_STEP, 256):
-            wide_ref[start : start + 256, :] = table_ref[start : start + 256, :].astype(jnp.float32)
-    index_copy.wait()
-
+    for start in range(0, items, 256):
+        wide_ref[start : start + 256, :] = table_ref[start : start + 256, :].astype(jnp.float32)
     sent = []
-    for device in range(devices):
-        rows = [wide_ref[pl.ds(index_ref[device, slot], 1), :] for slot in range(capacity)]
-        out_ref[device, :capacity, :] = jnp.concatenate(rows, axis=0).astype(jnp.bfloat16)
-        out_ref[device, capacity:, :] = tail
-        if (device + 1) % OUT_STEP == 0:
-            span = pl.ds(device + 1 - OUT_STEP, OUT_STEP)
-            sent.append(pltpu.make_async_copy(out_ref.at[span], out_hbm.at[span], out_sems.at[len(sent)]))
-            sent[-1].start()
+    for at in range(half):
+        if at % (half // INDEX_PIECES) == 0:
+            index_copies[at // (half // INDEX_PIECES)].wait()
+        for device, place in ((at, 0), (half + at, capacity)):
+            rows = [wide_ref[pl.ds(index_ref[at, place + slot], 1), :] for slot in range(capacity)]
+            out_ref[device, :capacity, :] = jnp.concatenate(rows, axis=0).astype(jnp.bfloat16)
+            out_ref[device, capacity:, :] = tail
+        if (at + 1) % OUT_STEP == 0:
+            for end in (at + 1, half + at + 1):
+                span = pl.ds(end - OUT_STEP, OUT_STEP)
+                sent.append(pltpu.make_async_copy(out_ref.at[span], out_hbm.at[span], out_sems.at[len(sent)]))
+                sent[-1].start()
     for copy in sent:
         copy.wait()
 
@@ -158,19 +159,17 @@
     return pl.pallas_call(
         fetch_kernel,
         out_shape=jax.ShapeDtypeStruct((devices, capacity + TAIL, features), jnp.bfloat16),
-        in_specs=[vmem, pl.BlockSpec(memory_space=pl.ANY)],
+        in_specs=[vmem, vmem],
         out_specs=pl.BlockSpec(memory_space=pl.ANY),
         scratch_shapes=[
-            pltpu.VMEM((items, features), jnp.bfloat16),
             pltpu.VMEM((items, features), jnp.float32),
-            pltpu.VMEM((devices, 2 * capacity), jnp.int32),
-            pltpu.SMEM((devices, 2 * capacity), jnp.int32),
+            pltpu.VMEM((devices // 2, 2 * capacity), jnp.int32),
+            pltpu.SMEM((devices // 2, 2 * capacity), jnp.int32),
             pltpu.VMEM((devices, capacity + TAIL, features), jnp.bfloat16),
-            pltpu.SemaphoreType.DMA((items // TABLE_STEP,)),
-            pltpu.SemaphoreType.DMA,
+            pltpu.SemaphoreType.DMA((INDEX_PIECES,)),
             pltpu.SemaphoreType.DMA((devices // OUT_STEP,)),
         ],
-        compiler_params=pltpu.CompilerParams(vmem_limit_bytes=VMEM_LIMIT),
+        compiler_params=pltpu.CompilerParams(vmem_limit_bytes=FETCH_LIMIT),
         cost_estimate=pl.CostEstimate(flops=0, bytes_accessed=24 * 2**20, transcendentals=0),
     )(received, item_table)
 
@@ -182,10 +181,24 @@
 
 
 def solve_kernel(
-    total_items, slots_ref, arrived_ref, weights_ref, counts_ref, start_ref, out_ref, wide_ref, shared_ref, conf_ref, system_ref
+    total_items,
+    slots_hbm,
+    arrived_ref,
+    weights_ref,
+    counts_ref,
+    start_ref,
+    out_ref,
+    wide_ref,
+    shared_ref,
+    conf_ref,
+    system_ref,
+    slots_ref,
+    slots_sem,
 ):
     users, links = slots_ref.shape
     devices, held, features = arrived_ref.shape
+    slots_copy = pltpu.make_async_copy(slots_hbm, slots_ref, slots_sem)
+    slots_copy.start()
     capacity = held - TAIL
 
     def widen(device, carry):
@@ -265,6 +278,7 @@
     estimate = jnp.concatenate([start_rows, start_rows], axis=0).T
     operand = stationary(estimate)
     zero = jnp.zeros((features, 2 * users), jnp.float32)
+    slots_copy.wait()
     chains, last = [], 0
     for batch in BATCHES:
         first, last = last, last + batch
@@ -287,13 +301,15 @@
     return pl.pallas_call(
         functools.partial(solve_kernel, total_items),
         out_shape=jax.ShapeDtypeStruct((users, features), jnp.float32),
-        in_specs=[pl.BlockSpec(memory_space=pltpu.SMEM)] + [vmem] * 4,
+        in_specs=[pl.BlockSpec(memory_space=pl.ANY)] + [vmem] * 4,
         out_specs=vmem,
         scratch_shapes=[
             pltpu.VMEM((users * links, features), jnp.float32),
             pltpu.VMEM((features, features), jnp.float32),
             pltpu.VMEM((users, links), jnp.float32),
             pltpu.VMEM((users * features, 2 * features), jnp.bfloat16),
+            pltpu.SMEM((users, links), jnp.int32),
+            pltpu.SemaphoreType.DMA,
         ],
         compiler_params=pltpu.CompilerParams(vmem_limit_bytes=SOLVE_LIMIT),
         cost_estimate=pl.CostEstimate(flops=2**32, bytes_accessed=24 * 2**20, transcendentals=0),

time: 84 us -> 81.1 us (0.965)
  Pallas kernels: 24.2 us -> 21.6 us
    pallas_call x1, Pallas kernels: 8.35 us -> 6.06 us  [fetch_rows(): pl.pallas_call(fetch_kernel, out_shape=jax.ShapeDtypeStruct((devices, cap...]
where the time goes in v4:
time: 81.1 us; the launch traced here: 80.8 us
  waiting for transfers between devices  33.2 us (41%)
  Pallas kernels  21.6 us (27%)
  blocking collectives  21.5 us (27%)
  starting transfers between devices  4.12 us (5%)
    all_to_all x1, waiting for transfers between devices, exchange(): return lax.all_to_all(value, AXES, split_axis=0, concat_axis=0, tiled=True)  33.2 us
    all_to_all x1, blocking collectives, exchange(): return lax.all_to_all(value, AXES, split_axis=0, concat_axis=0, tiled=True)  21.5 us
    pallas_call x1, Pallas kernels, solve_rows(): pl.pallas_call(functools.partial(solve_kernel, total_items), out_shape=ja...  11.1 us
    pallas_call x1, Pallas kernels, fetch_rows(): pl.pallas_call(fetch_kernel, out_shape=jax.ShapeDtypeStruct((devices, cap...  6.06 us
    pallas_call x1, Pallas kernels, ask(): pl.pallas_call(ask_kernel, out_shape=jax.ShapeDtypeStruct((devices, 1, 2...  4.5 us
    all_to_all x1, starting transfers between devices, exchange(): return lax.all_to_all(value, AXES, split_axis=0, concat_axis=0, tiled=True)  4.12 us
  transfers between devices with their start and end apart: 1, of which 1 were waited for; matrix products, arithmetic and copies ran while one was open for 0% of the time, Pallas kernels for 0%

profile of v4, /device:TPU:1, one launch (start us, length us, event | category | flops | bytes accessed | tf_op | source)
XLA Modules:
  0.0 80.8 jit_solution(13367133117001044486)
XLA Ops:
  0.0 0.0 copy-start
  0.0 4.5 %shard_map.64 = f32[128,1,256]{2,1,0:T(1,128)} custom-call(s32[64,128]{1,0:T(8,128)} %slots_hbm.3, s32[64,128]{1,0:T(8,128)} %rows_hbm.1, bf16[16384,128]{1,0:T(8,128)(2,1)} %table_ref.1), custom_call_target="tpu_custom_call" | custom-call | flops 1073741824 | bytes 4194304 | tf_op jit(solution)/shard_map/pallas_call | solution.py:101
  4.5 21.5 %all_to_all.10.received_ref = f32[128,1,256]{2,1,0:T(1,128)S(1)} all-to-all(f32[128,1,256]{2,1,0:T(1,128)} %shard_map.64), channel_id=1, replica_groups=mesh['rows'=16,'table'=8] {'rows','table'}, dimensions={0} | all-to-all | bytes 262144 | tf_op jit(solution)/shard_map/all_to_all | solution.py:320
  26.1 0.0 copy-done
  26.1 6.1 %shard_map.65 = bf16[128,72,128]{2,1,0:T(8,128)(2,1)} custom-call(f32[128,1,256]{2,1,0:T(1,128)S(1)} %all_to_all.10.received_ref, bf16[16384,128]{1,0:T(8,128)(2,1)S(1)} %copy-done), custom_call_target="tpu_custom_call" | custom-call | bytes 25165824 | tf_op jit(solution)/shard_map/pallas_call | solution.py:159
  32.1 0.0 copy-start.4
  32.1 0.0 copy-start.1
  32.1 0.0 copy-start.2
  32.2 0.0 copy-start.3
  32.2 4.1 %all-to-all-start.1 = ((bf16[128,72,128]{2,1,0:T(8,128)(2,1)}), bf16[128,72,128]{2,1,0:T(8,128)(2,1)S(1)}, u32[]{:S(2)}, u32[]{:S(2)}) async-start(bf16[128,72,128]{2,1,0:T(8,128)(2,1)} %shard_map.65), calls=%async_computation.1 | async-start | bytes 4718592 | tf_op jit(solution)/shard_map/all_to_all | solution.py:320
  36.3 0.0 copy-done.4
  36.3 0.1 copy.7.counts_ref
  36.4 33.2 %all-to-all-done.1.arrived_ref = bf16[128,72,128]{2,1,0:T(8,128)(2,1)S(1)} async-done(((bf16[128,72,128]{2,1,0:T(8,128)(2,1)}), bf16[128,72,128]{2,1,0:T(8,128)(2,1)S(1)}, u32[]{:S(2)}, u32[]{:S(2)}) %all-to-all-start.1) | async-done | bytes 2359328 | tf_op jit(solution)/shard_map/all_to_all | solution.py:320
  69.6 0.0 copy-done.1
  69.6 0.0 copy-done.2
  69.6 0.0 copy-done.3
  69.6 11.1 %shard_map.66 = f32[64,128]{1,0:T(8,128)} custom-call(s32[64,128]{1,0:T(8,128)S(1)} %copy-done.1, bf16[128,72,128]{2,1,0:T(8,128)(2,1)S(1)} %all-to-all-done.1.arrived_ref, s32[64,128]{1,0:T(8,128)S(1)} %copy-done.2, s32[64,1]{1,0:T(8,128)S(1)} %copy.7.counts_ref, f32[64,128]{1,0:T(8,128)S(1)} %copy-done.3), custom_call_target="tpu_custom_call" | custom-call | flops 4294967296 | bytes 25165824 | tf_op jit(solution)/shard_map/pallas_call | solution.py:301
Async XLA Ops:
  0.0 26.1 %copy-start = (bf16[16384,128]{1,0:T(8,128)(2,1)S(1)}, bf16[16384,128]{1,0:T(8,128)(2,1)}, u32[]{:S(2)}) copy-start(bf16[16384,128]{1,0:T(8,128)(2,1)} %table_ref.1) | copy-start | bytes 12582916
  32.1 4.2 %copy-start.4 = (s32[64]{0:T(128)S(1)}, s32[64]{0:T(128)}, u32[]{:S(2)}) copy-start(s32[64]{0:T(128)} %param.11) | copy-start | bytes 772
  32.1 37.5 %copy-start.1 = (s32[64,128]{1,0:T(8,128)S(1)}, s32[64,128]{1,0:T(8,128)}, u32[]{:S(2)}) copy-start(s32[64,128]{1,0:T(8,128)} %slots_hbm.3) | copy-start | bytes 98308
  32.1 37.5 %copy-start.2 = (s32[64,128]{1,0:T(8,128)S(1)}, s32[64,128]{1,0:T(8,128)}, u32[]{:S(2)}) copy-start(s32[64,128]{1,0:T(8,128)} %weights_ref.1) | copy-start | bytes 98308
  32.2 37.4 %copy-start.3 = (f32[64,128]{1,0:T(8,128)S(1)}, f32[64,128]{1,0:T(8,128)}, u32[]{:S(2)}) copy-start(f32[64,128]{1,0:T(8,128)} %start_ref.1) | copy-start | bytes 98308
  32.2 37.4 %all-to-all-start.1 = ((bf16[128,72,128]{2,1,0:T(8,128)(2,1)}), bf16[128,72,128]{2,1,0:T(8,128)(2,1)S(1)}, u32[]{:S(2)}, u32[]{:S(2)}) async-start(bf16[128,72,128]{2,1,0:T(8,128)(2,1)} %shard_map.65), calls=%async_computation.1 | async-start | bytes 4718592 | tf_op jit(solution)/shard_map/all_to_all | solution.py:320

commit v5 on v4

--- a/solution.py
+++ b/solution.py
@@ -9,7 +9,8 @@
 
 CG_STEPS = 3
 BATCHES = (32, 32)
-TOGETHER = 4
+TOGETHER = 8
+FORMED = 16
 AXES = ("rows", "table")
 VMEM_LIMIT = 56 * 2**20
 FETCH_LIMIT = 24 * 2**20
@@ -220,7 +221,7 @@
     conf_ref[...] = jnp.where(
         link_id < counts_ref[...], 1.0 + weights_ref[...].astype(jnp.float32) / 8.0, 0.0
     )
-    lane = lax.broadcasted_iota(jnp.int32, (features, 2 * users), 1)
+    lane = lax.broadcasted_iota(jnp.int32, (1, 2 * users), 1)
     user_lane = jnp.where(lane < users, lane, lane - users)
     ones = jnp.ones((links, 2 * users), jnp.bfloat16)
 
@@ -232,7 +233,7 @@
     def both_halves(image):
         return image + pltpu.roll(image, users, 1)
 
-    def form(user, operand, target, image):
+    def form(user, target):
         rows = [wide_ref[pl.ds(slots_ref[user, link], 1), :] for link in range(links)]
         fetched = jnp.concatenate(rows, axis=0)
         scaled = (fetched.T * conf_ref[user : user + 1, :]).astype(jnp.bfloat16)
@@ -243,9 +244,16 @@
         )
         system = jnp.concatenate(split(both[:, :features] + shared_ref[...]), axis=1)
         system_ref[user * features : (user + 1) * features, :] = system
-        first = jnp.dot(system, operand, preferred_element_type=jnp.float32)
-        mine = user_lane == user
-        return jnp.where(mine, both[:, features:], target), jnp.where(mine, first, image)
+        return jnp.where(user_lane == user, both[:, features:], target)
+
+    def apply_some(user, count, operand, image):
+        product = jnp.dot(
+            system_ref[user * features : (user + count) * features, :], operand, preferred_element_type=jnp.float32
+        )
+        for one in range(count):
+            piece = product[one * features : (one + 1) * features]
+            image = jnp.where(user_lane == user + one, piece, image)
+        return image
 
     def refine(first, last, target, image, estimate):
         residual = target - both_halves(image)
@@ -255,14 +263,7 @@
             operand = stationary(direction)
             image = jnp.zeros_like(direction)
             for user in range(first, last, TOGETHER):
-                product = jnp.dot(
-                    system_ref[user * features : (user + TOGETHER) * features, :],
-                    operand,
-                    preferred_element_type=jnp.float32,
-                )
-                for one in range(TOGETHER):
-                    piece = product[one * features : (one + 1) * features]
-                    image = jnp.where(user_lane == user + one, piece, image)
+                image = apply_some(user, TOGETHER, operand, image)
             yield None
             image = both_halves(image)
             curvature = jnp.sum(direction * image, axis=0, keepdims=True)
@@ -284,7 +285,9 @@
         first, last = last, last + batch
         target, image = zero, zero
         for user in range(first, last):
-            target, image = form(user, operand, target, image)
+            target = form(user, target)
+            if (user + 1) % FORMED == 0:
+                image = apply_some(user + 1 - FORMED, FORMED, operand, image)
         chains.append(refine(first, last, target, image, estimate if not chains else zero))
     total = zero
     for _ in range(CG_STEPS + 1):

time: 81.1 us -> 80.8 us (level)
  no operation moved by 1% of the time
where the time goes in v5:
time: 80.8 us; the launch traced here: 80.6 us
  waiting for transfers between devices  33.2 us (41%)
  blocking collectives  21.5 us (27%)
  Pallas kernels  21.4 us (26%)
  starting transfers between devices  4.12 us (5%)
    all_to_all x1, waiting for transfers between devices, exchange(): return lax.all_to_all(value, AXES, split_axis=0, concat_axis=0, tiled=True)  33.2 us
    all_to_all x1, blocking collectives, exchange(): return lax.all_to_all(value, AXES, split_axis=0, concat_axis=0, tiled=True)  21.5 us
    pallas_call x1, Pallas kernels, solve_rows(): pl.pallas_call(functools.partial(solve_kernel, total_items), out_shape=ja...  10.8 us
    pallas_call x1, Pallas kernels, fetch_rows(): pl.pallas_call(fetch_kernel, out_shape=jax.ShapeDtypeStruct((devices, cap...  6.06 us
    pallas_call x1, Pallas kernels, ask(): pl.pallas_call(ask_kernel, out_shape=jax.ShapeDtypeStruct((devices, 1, 2...  4.5 us
    all_to_all x1, starting transfers between devices, exchange(): return lax.all_to_all(value, AXES, split_axis=0, concat_axis=0, tiled=True)  4.12 us
  transfers between devices with their start and end apart: 1, of which 1 were waited for; matrix products, arithmetic and copies ran while one was open for 0% of the time, Pallas kernels for 0%

profile of v5, /device:TPU:1, one launch (start us, length us, event | category | flops | bytes accessed | tf_op | source)
XLA Modules:
  0.0 80.6 jit_solution(7126961849897979248)
XLA Ops:
  0.0 0.0 copy-start
  0.0 4.5 %shard_map.64 = f32[128,1,256]{2,1,0:T(1,128)} custom-call(s32[64,128]{1,0:T(8,128)} %slots_hbm.3, s32[64,128]{1,0:T(8,128)} %rows_hbm.1, bf16[16384,128]{1,0:T(8,128)(2,1)} %table_ref.1), custom_call_target="tpu_custom_call" | custom-call | flops 1073741824 | bytes 4194304 | tf_op jit(solution)/shard_map/pallas_call | solution.py:102
  4.5 21.5 %all_to_all.10.received_ref = f32[128,1,256]{2,1,0:T(1,128)S(1)} all-to-all(f32[128,1,256]{2,1,0:T(1,128)} %shard_map.64), channel_id=1, replica_groups=mesh['rows'=16,'table'=8] {'rows','table'}, dimensions={0} | all-to-all | bytes 262144 | tf_op jit(solution)/shard_map/all_to_all | solution.py:323
  26.1 0.0 copy-done
  26.1 6.1 %shard_map.65 = bf16[128,72,128]{2,1,0:T(8,128)(2,1)} custom-call(f32[128,1,256]{2,1,0:T(1,128)S(1)} %all_to_all.10.received_ref, bf16[16384,128]{1,0:T(8,128)(2,1)S(1)} %copy-done), custom_call_target="tpu_custom_call" | custom-call | bytes 25165824 | tf_op jit(solution)/shard_map/pallas_call | solution.py:160
  32.1 0.0 copy-start.4
  32.1 0.0 copy-start.1
  32.1 0.0 copy-start.2
  32.2 0.0 copy-start.3
  32.2 4.1 %all-to-all-start.1 = ((bf16[128,72,128]{2,1,0:T(8,128)(2,1)}), bf16[128,72,128]{2,1,0:T(8,128)(2,1)S(1)}, u32[]{:S(2)}, u32[]{:S(2)}) async-start(bf16[128,72,128]{2,1,0:T(8,128)(2,1)} %shard_map.65), calls=%async_computation.1 | async-start | bytes 4718592 | tf_op jit(solution)/shard_map/all_to_all | solution.py:323
  36.3 0.0 copy-done.4
  36.3 0.1 copy.7.counts_ref
  36.4 33.2 %all-to-all-done.1.arrived_ref = bf16[128,72,128]{2,1,0:T(8,128)(2,1)S(1)} async-done(((bf16[128,72,128]{2,1,0:T(8,128)(2,1)}), bf16[128,72,128]{2,1,0:T(8,128)(2,1)S(1)}, u32[]{:S(2)}, u32[]{:S(2)}) %all-to-all-start.1) | async-done | bytes 2359328 | tf_op jit(solution)/shard_map/all_to_all | solution.py:323
  69.6 0.0 copy-done.1
  69.6 0.0 copy-done.2
  69.6 0.0 copy-done.3
  69.6 10.8 %shard_map.66 = f32[64,128]{1,0:T(8,128)} custom-call(s32[64,128]{1,0:T(8,128)S(1)} %copy-done.1, bf16[128,72,128]{2,1,0:T(8,128)(2,1)S(1)} %all-to-all-done.1.arrived_ref, s32[64,128]{1,0:T(8,128)S(1)} %copy-done.2, s32[64,1]{1,0:T(8,128)S(1)} %copy.7.counts_ref, f32[64,128]{1,0:T(8,128)S(1)} %copy-done.3), custom_call_target="tpu_custom_call" | custom-call | flops 4294967296 | bytes 25165824 | tf_op jit(solution)/shard_map/pallas_call | solution.py:304
Async XLA Ops:
  0.0 26.1 %copy-start = (bf16[16384,128]{1,0:T(8,128)(2,1)S(1)}, bf16[16384,128]{1,0:T(8,128)(2,1)}, u32[]{:S(2)}) copy-start(bf16[16384,128]{1,0:T(8,128)(2,1)} %table_ref.1) | copy-start | bytes 12582916
  32.1 4.2 %copy-start.4 = (s32[64]{0:T(128)S(1)}, s32[64]{0:T(128)}, u32[]{:S(2)}) copy-start(s32[64]{0:T(128)} %param.11) | copy-start | bytes 772
  32.1 37.5 %copy-start.1 = (s32[64,128]{1,0:T(8,128)S(1)}, s32[64,128]{1,0:T(8,128)}, u32[]{:S(2)}) copy-start(s32[64,128]{1,0:T(8,128)} %slots_hbm.3) | copy-start | bytes 98308
  32.1 37.5 %copy-start.2 = (s32[64,128]{1,0:T(8,128)S(1)}, s32[64,128]{1,0:T(8,128)}, u32[]{:S(2)}) copy-start(s32[64,128]{1,0:T(8,128)} %weights_ref.1) | copy-start | bytes 98308
  32.2 37.4 %copy-start.3 = (f32[64,128]{1,0:T(8,128)S(1)}, f32[64,128]{1,0:T(8,128)}, u32[]{:S(2)}) copy-start(f32[64,128]{1,0:T(8,128)} %start_ref.1) | copy-start | bytes 98308
  32.2 37.4 %all-to-all-start.1 = ((bf16[128,72,128]{2,1,0:T(8,128)(2,1)}), bf16[128,72,128]{2,1,0:T(8,128)(2,1)S(1)}, u32[]{:S(2)}, u32[]{:S(2)}) async-start(bf16[128,72,128]{2,1,0:T(8,128)(2,1)} %shard_map.65), calls=%async_computation.1 | async-start | bytes 4718592 | tf_op jit(solution)/shard_map/all_to_all | solution.py:323

commit v6 on v5

--- a/solution.py
+++ b/solution.py
@@ -18,7 +18,6 @@
 NT = (((1,), (1,)), ((), ()))
 TN = (((0,), (0,)), ((), ()))
 TABLE_STEP = 2048
-OUT_STEP = 8
 INDEX_PIECES = 4
 PLACE_FIRST = 32
 TAIL = 8
@@ -115,7 +114,7 @@
     )(link_slots, link_rows, item_table)
 
 
-def fetch_kernel(received_ref, table_ref, out_hbm, wide_ref, index_vmem, index_ref, out_ref, index_sems, out_sems):
+def fetch_kernel(received_ref, table_ref, out_ref, wide_ref, index_vmem, index_ref, index_sems):
     items, features = table_ref.shape
     devices, held, _ = out_ref.shape
     capacity = held - TAIL
@@ -136,7 +135,6 @@
     tail = jnp.concatenate(terms + [jnp.zeros((TAIL - 3, features), jnp.float32)], axis=0).astype(jnp.bfloat16)
     for start in range(0, items, 256):
         wide_ref[start : start + 256, :] = table_ref[start : start + 256, :].astype(jnp.float32)
-    sent = []
     for at in range(half):
         if at % (half // INDEX_PIECES) == 0:
             index_copies[at // (half // INDEX_PIECES)].wait()
@@ -144,13 +142,6 @@
             rows = [wide_ref[pl.ds(index_ref[at, place + slot], 1), :] for slot in range(capacity)]
             out_ref[device, :capacity, :] = jnp.concatenate(rows, axis=0).astype(jnp.bfloat16)
             out_ref[device, capacity:, :] = tail
-        if (at + 1) % OUT_STEP == 0:
-            for end in (at + 1, half + at + 1):
-                span = pl.ds(end - OUT_STEP, OUT_STEP)
-                sent.append(pltpu.make_async_copy(out_ref.at[span], out_hbm.at[span], out_sems.at[len(sent)]))
-                sent[-1].start()
-    for copy in sent:
-        copy.wait()
 
 
 def fetch_rows(received, item_table, capacity):
@@ -161,14 +152,12 @@
         fetch_kernel,
         out_shape=jax.ShapeDtypeStruct((devices, capacity + TAIL, features), jnp.bfloat16),
         in_specs=[vmem, vmem],
-        out_specs=pl.BlockSpec(memory_space=pl.ANY),
+        out_specs=vmem,
         scratch_shapes=[
             pltpu.VMEM((items, features), jnp.float32),
             pltpu.VMEM((devices // 2, 2 * capacity), jnp.int32),
             pltpu.SMEM((devices // 2, 2 * capacity), jnp.int32),
-            pltpu.VMEM((devices, capacity + TAIL, features), jnp.bfloat16),
             pltpu.SemaphoreType.DMA((INDEX_PIECES,)),
-            pltpu.SemaphoreType.DMA((devices // OUT_STEP,)),
         ],
         compiler_params=pltpu.CompilerParams(vmem_limit_bytes=FETCH_LIMIT),
         cost_estimate=pl.CostEstimate(flops=0, bytes_accessed=24 * 2**20, transcendentals=0),

time: 80.8 us -> 81.3 us (level)
  no operation moved by 1% of the time
where the time goes in v6:
time: 81.3 us; the launch traced here: 81.1 us
  waiting for transfers between devices  33.2 us (41%)
  Pallas kernels  21.9 us (27%)
  blocking collectives  21.5 us (26%)
  starting transfers between devices  4.12 us (5%)
    all_to_all x1, waiting for transfers between devices, exchange(): return lax.all_to_all(value, AXES, split_axis=0, concat_axis=0, tiled=True)  33.2 us
    all_to_all x1, blocking collectives, exchange(): return lax.all_to_all(value, AXES, split_axis=0, concat_axis=0, tiled=True)  21.5 us
    pallas_call x1, Pallas kernels, solve_rows(): pl.pallas_call(functools.partial(solve_kernel, total_items), out_shape=ja...  10.8 us
    pallas_call x1, Pallas kernels, fetch_rows(): pl.pallas_call(fetch_kernel, out_shape=jax.ShapeDtypeStruct((devices, cap...  6.59 us
    pallas_call x1, Pallas kernels, ask(): pl.pallas_call(ask_kernel, out_shape=jax.ShapeDtypeStruct((devices, 1, 2...  4.5 us
    all_to_all x1, starting transfers between devices, exchange(): return lax.all_to_all(value, AXES, split_axis=0, concat_axis=0, tiled=True)  4.12 us
  transfers between devices with their start and end apart: 1, of which 1 were waited for; matrix products, arithmetic and copies ran while one was open for 0% of the time, Pallas kernels for 0%

profile of v6, /device:TPU:1, one launch (start us, length us, event | category | flops | bytes accessed | tf_op | source)
XLA Modules:
  0.0 81.1 jit_solution(6132639837347767436)
XLA Ops:
  0.0 0.0 copy-start
  0.0 4.5 %shard_map.64 = f32[128,1,256]{2,1,0:T(1,128)} custom-call(s32[64,128]{1,0:T(8,128)} %slots_hbm.3, s32[64,128]{1,0:T(8,128)} %rows_hbm.1, bf16[16384,128]{1,0:T(8,128)(2,1)} %table_ref.1), custom_call_target="tpu_custom_call" | custom-call | flops 1073741824 | bytes 4194304 | tf_op jit(solution)/shard_map/pallas_call | solution.py:101
  4.5 21.5 %all_to_all.10.received_ref = f32[128,1,256]{2,1,0:T(1,128)S(1)} all-to-all(f32[128,1,256]{2,1,0:T(1,128)} %shard_map.64), channel_id=1, replica_groups=mesh['rows'=16,'table'=8] {'rows','table'}, dimensions={0} | all-to-all | bytes 262144 | tf_op jit(solution)/shard_map/all_to_all | solution.py:312
  26.1 0.0 copy-done
  26.1 6.6 %shard_map.65 = bf16[128,72,128]{2,1,0:T(8,128)(2,1)} custom-call(f32[128,1,256]{2,1,0:T(1,128)S(1)} %all_to_all.10.received_ref, bf16[16384,128]{1,0:T(8,128)(2,1)S(1)} %copy-done), custom_call_target="tpu_custom_call" | custom-call | bytes 25165824 | tf_op jit(solution)/shard_map/pallas_call | solution.py:151
  32.6 0.0 copy-start.4
  32.7 0.0 copy-start.1
  32.7 0.0 copy-start.2
  32.7 0.0 copy-start.3
  32.7 4.1 %all-to-all-start.1 = ((bf16[128,72,128]{2,1,0:T(8,128)(2,1)}), bf16[128,72,128]{2,1,0:T(8,128)(2,1)S(1)}, u32[]{:S(2)}, u32[]{:S(2)}) async-start(bf16[128,72,128]{2,1,0:T(8,128)(2,1)} %shard_map.65), calls=%async_computation.1 | async-start | bytes 4718592 | tf_op jit(solution)/shard_map/all_to_all | solution.py:312
  36.8 0.0 copy-done.4
  36.8 0.1 copy.7.counts_ref
  36.9 33.2 %all-to-all-done.1.arrived_ref = bf16[128,72,128]{2,1,0:T(8,128)(2,1)S(1)} async-done(((bf16[128,72,128]{2,1,0:T(8,128)(2,1)}), bf16[128,72,128]{2,1,0:T(8,128)(2,1)S(1)}, u32[]{:S(2)}, u32[]{:S(2)}) %all-to-all-start.1) | async-done | bytes 2359328 | tf_op jit(solution)/shard_map/all_to_all | solution.py:312
  70.1 0.0 copy-done.1
  70.1 0.0 copy-done.2
  70.1 0.0 copy-done.3
  70.1 10.8 %shard_map.66 = f32[64,128]{1,0:T(8,128)} custom-call(s32[64,128]{1,0:T(8,128)S(1)} %copy-done.1, bf16[128,72,128]{2,1,0:T(8,128)(2,1)S(1)} %all-to-all-done.1.arrived_ref, s32[64,128]{1,0:T(8,128)S(1)} %copy-done.2, s32[64,1]{1,0:T(8,128)S(1)} %copy.7.counts_ref, f32[64,128]{1,0:T(8,128)S(1)} %copy-done.3), custom_call_target="tpu_custom_call" | custom-call | flops 4294967296 | bytes 25165824 | tf_op jit(solution)/shard_map/pallas_call | solution.py:293
Async XLA Ops:
  0.0 26.1 %copy-start = (bf16[16384,128]{1,0:T(8,128)(2,1)S(1)}, bf16[16384,128]{1,0:T(8,128)(2,1)}, u32[]{:S(2)}) copy-start(bf16[16384,128]{1,0:T(8,128)(2,1)} %table_ref.1) | copy-start | bytes 12582916
  32.6 4.2 %copy-start.4 = (s32[64]{0:T(128)S(1)}, s32[64]{0:T(128)}, u32[]{:S(2)}) copy-start(s32[64]{0:T(128)} %param.11) | copy-start | bytes 772
  32.7 37.5 %copy-start.1 = (s32[64,128]{1,0:T(8,128)S(1)}, s32[64,128]{1,0:T(8,128)}, u32[]{:S(2)}) copy-start(s32[64,128]{1,0:T(8,128)} %slots_hbm.3) | copy-start | bytes 98308
  32.7 37.5 %copy-start.2 = (s32[64,128]{1,0:T(8,128)S(1)}, s32[64,128]{1,0:T(8,128)}, u32[]{:S(2)}) copy-start(s32[64,128]{1,0:T(8,128)} %weights_ref.1) | copy-start | bytes 98308
  32.7 37.4 %copy-start.3 = (f32[64,128]{1,0:T(8,128)S(1)}, f32[64,128]{1,0:T(8,128)}, u32[]{:S(2)}) copy-start(f32[64,128]{1,0:T(8,128)} %start_ref.1) | copy-start | bytes 98308
  32.7 37.4 %all-to-all-start.1 = ((bf16[128,72,128]{2,1,0:T(8,128)(2,1)}), bf16[128,72,128]{2,1,0:T(8,128)(2,1)S(1)}, u32[]{:S(2)}, u32[]{:S(2)}) async-start(bf16[128,72,128]{2,1,0:T(8,128)(2,1)} %shard_map.65), calls=%async_computation.1 | async-start | bytes 4718592 | tf_op jit(solution)/shard_map/all_to_all | solution.py:312

commit v7 on v5

--- a/solution.py
+++ b/solution.py
@@ -209,7 +209,7 @@
         shared_ref[pl.ds(device, 1), :] = jnp.sum(tail, axis=0, keepdims=True)
         return carry
 
-    lax.fori_loop(0, devices, widen, 0, unroll=8)
+    lax.fori_loop(0, devices, widen, 0, unroll=32)
     diagonal = jnp.where(
         lax.broadcasted_iota(jnp.int32, (features, features), 0)
         == lax.broadcasted_iota(jnp.int32, (features, features), 1),

time: 80.8 us -> 80.8 us (level)
  no operation moved by 1% of the time
where the time goes in v7:
time: 80.8 us; the launch traced here: 80.6 us
  waiting for transfers between devices  33.2 us (41%)
  blocking collectives  21.5 us (27%)
  Pallas kernels  21.4 us (26%)
  starting transfers between devices  4.12 us (5%)
    all_to_all x1, waiting for transfers between devices, exchange(): return lax.all_to_all(value, AXES, split_axis=0, concat_axis=0, tiled=True)  33.2 us
    all_to_all x1, blocking collectives, exchange(): return lax.all_to_all(value, AXES, split_axis=0, concat_axis=0, tiled=True)  21.5 us
    pallas_call x1, Pallas kernels, solve_rows(): pl.pallas_call(functools.partial(solve_kernel, total_items), out_shape=ja...  10.8 us
    pallas_call x1, Pallas kernels, fetch_rows(): pl.pallas_call(fetch_kernel, out_shape=jax.ShapeDtypeStruct((devices, cap...  6.06 us
    pallas_call x1, Pallas kernels, ask(): pl.pallas_call(ask_kernel, out_shape=jax.ShapeDtypeStruct((devices, 1, 2...  4.5 us
    all_to_all x1, starting transfers between devices, exchange(): return lax.all_to_all(value, AXES, split_axis=0, concat_axis=0, tiled=True)  4.12 us
  transfers between devices with their start and end apart: 1, of which 1 were waited for; matrix products, arithmetic and copies ran while one was open for 0% of the time, Pallas kernels for 0%

profile of v7, /device:TPU:1, one launch (start us, length us, event | category | flops | bytes accessed | tf_op | source)
XLA Modules:
  0.0 80.6 jit_solution(1164268097052693746)
XLA Ops:
  0.0 0.0 copy-start
  0.0 4.5 %shard_map.64 = f32[128,1,256]{2,1,0:T(1,128)} custom-call(s32[64,128]{1,0:T(8,128)} %slots_hbm.3, s32[64,128]{1,0:T(8,128)} %rows_hbm.1, bf16[16384,128]{1,0:T(8,128)(2,1)} %table_ref.1), custom_call_target="tpu_custom_call" | custom-call | flops 1073741824 | bytes 4194304 | tf_op jit(solution)/shard_map/pallas_call | solution.py:102
  4.5 21.5 %all_to_all.10.received_ref = f32[128,1,256]{2,1,0:T(1,128)S(1)} all-to-all(f32[128,1,256]{2,1,0:T(1,128)} %shard_map.64), channel_id=1, replica_groups=mesh['rows'=16,'table'=8] {'rows','table'}, dimensions={0} | all-to-all | bytes 262144 | tf_op jit(solution)/shard_map/all_to_all | solution.py:323
  26.1 0.0 copy-done
  26.1 6.1 %shard_map.65 = bf16[128,72,128]{2,1,0:T(8,128)(2,1)} custom-call(f32[128,1,256]{2,1,0:T(1,128)S(1)} %all_to_all.10.received_ref, bf16[16384,128]{1,0:T(8,128)(2,1)S(1)} %copy-done), custom_call_target="tpu_custom_call" | custom-call | bytes 25165824 | tf_op jit(solution)/shard_map/pallas_call | solution.py:160
  32.1 0.0 copy-start.4
  32.1 0.0 copy-start.1
  32.1 0.0 copy-start.2
  32.2 0.0 copy-start.3
  32.2 4.1 %all-to-all-start.1 = ((bf16[128,72,128]{2,1,0:T(8,128)(2,1)}), bf16[128,72,128]{2,1,0:T(8,128)(2,1)S(1)}, u32[]{:S(2)}, u32[]{:S(2)}) async-start(bf16[128,72,128]{2,1,0:T(8,128)(2,1)} %shard_map.65), calls=%async_computation.1 | async-start | bytes 4718592 | tf_op jit(solution)/shard_map/all_to_all | solution.py:323
  36.3 0.0 copy-done.4
  36.3 0.1 copy.7.counts_ref
  36.4 33.2 %all-to-all-done.1.arrived_ref = bf16[128,72,128]{2,1,0:T(8,128)(2,1)S(1)} async-done(((bf16[128,72,128]{2,1,0:T(8,128)(2,1)}), bf16[128,72,128]{2,1,0:T(8,128)(2,1)S(1)}, u32[]{:S(2)}, u32[]{:S(2)}) %all-to-all-start.1) | async-done | bytes 2359328 | tf_op jit(solution)/shard_map/all_to_all | solution.py:323
  69.6 0.0 copy-done.1
  69.6 0.0 copy-done.2
  69.6 0.0 copy-done.3
  69.6 10.8 %shard_map.66 = f32[64,128]{1,0:T(8,128)} custom-call(s32[64,128]{1,0:T(8,128)S(1)} %copy-done.1, bf16[128,72,128]{2,1,0:T(8,128)(2,1)S(1)} %all-to-all-done.1.arrived_ref, s32[64,128]{1,0:T(8,128)S(1)} %copy-done.2, s32[64,1]{1,0:T(8,128)S(1)} %copy.7.counts_ref, f32[64,128]{1,0:T(8,128)S(1)} %copy-done.3), custom_call_target="tpu_custom_call" | custom-call | flops 4294967296 | bytes 25165824 | tf_op jit(solution)/shard_map/pallas_call | solution.py:304
Async XLA Ops:
  0.0 26.1 %copy-start = (bf16[16384,128]{1,0:T(8,128)(2,1)S(1)}, bf16[16384,128]{1,0:T(8,128)(2,1)}, u32[]{:S(2)}) copy-start(bf16[16384,128]{1,0:T(8,128)(2,1)} %table_ref.1) | copy-start | bytes 12582916
  32.1 4.2 %copy-start.4 = (s32[64]{0:T(128)S(1)}, s32[64]{0:T(128)}, u32[]{:S(2)}) copy-start(s32[64]{0:T(128)} %param.11) | copy-start | bytes 772
  32.1 37.5 %copy-start.1 = (s32[64,128]{1,0:T(8,128)S(1)}, s32[64,128]{1,0:T(8,128)}, u32[]{:S(2)}) copy-start(s32[64,128]{1,0:T(8,128)} %slots_hbm.3) | copy-start | bytes 98308
  32.1 37.5 %copy-start.2 = (s32[64,128]{1,0:T(8,128)S(1)}, s32[64,128]{1,0:T(8,128)}, u32[]{:S(2)}) copy-start(s32[64,128]{1,0:T(8,128)} %weights_ref.1) | copy-start | bytes 98308
  32.2 37.4 %copy-start.3 = (f32[64,128]{1,0:T(8,128)S(1)}, f32[64,128]{1,0:T(8,128)}, u32[]{:S(2)}) copy-start(f32[64,128]{1,0:T(8,128)} %start_ref.1) | copy-start | bytes 98308
  32.2 37.4 %all-to-all-start.1 = ((bf16[128,72,128]{2,1,0:T(8,128)(2,1)}), bf16[128,72,128]{2,1,0:T(8,128)(2,1)S(1)}, u32[]{:S(2)}, u32[]{:S(2)}) async-start(bf16[128,72,128]{2,1,0:T(8,128)(2,1)} %shard_map.65), calls=%async_computation.1 | async-start | bytes 4718592 | tf_op jit(solution)/shard_map/all_to_all | solution.py:323
